TPU v7x, 256 devices: a whole 4x4x8 slice. The times are simulated.
256 devices in a mesh: section: 8 (over z), dp: 8 (over y, x_lo), mp: 4 (over x_hi, core).
Axes of the slice: x: 4 (x_hi: 2, x_lo: 2; x = x_hi * 2 + x_lo), y: 4, z: 8, core: 2. Of those that a mesh axis runs over, the one named last changes fastest.
Arguments:
- enc_input: bfloat16 [4, 8, 16, 4096], P(None, 'dp', None, 'mp'), may hold values from -6 to 6
- dec_input: bfloat16 [4, 8, 16, 4096], P(None, 'dp', None, 'mp'), may hold values from -6 to 6
- cotangent: bfloat16 [4, 8, 16, 4096], P(None, 'dp', None, 'mp'), may hold values from -6 to 6
- target_lengths: int32 [4, 8], P(None, 'dp'), may hold values from 1 to 16, 96 in all within a row
- weights: bfloat16 [8, 4, 4096, 2048], P('section', None, 'dp', 'mp'), may hold values from -0.09375 to 0.09375
Outputs:
- weight_grads: float32 [8, 4, 4096, 2048], P('section', None, 'dp', 'mp')
Inputs may be any that keep to these rules, and one draw needn't show every extreme that they name: `target_lengths`: in every micro-batch the 8 lengths sum to 96 and the largest is 16.
All inputs are finite; a program needn't handle non-finite values. No bound on the sum of `target_lengths` on one device may be relied on, other than what follows from the above.
Results may differ from a plain program's by a relative error of at most 0.039.
Values may be sent and summed in bfloat16 or wider, within the bound.
A program may use at most 128 MiB of HBM per device.

v0:
```python
import jax
import jax.numpy as jnp
from jax import lax
from jax.sharding import PartitionSpec as P

HEAD_DIM = 256


epsilon = 1e-06


def passed_along(value, axis, by):
    size = lax.axis_size(axis)
    pairs = [(i, i + by) for i in range(size) if 0 <= i + by < size]
    return lax.ppermute(value, axis, pairs)


def normalize(values_in):
    widened = values_in.astype(jnp.float32)
    factor = lax.rsqrt(jnp.mean(widened * widened, axis=-1, keepdims=True) + epsilon)
    return (widened * factor, factor)


def norm_back(normed, factor, incoming):
    return factor * (incoming - normed * jnp.mean(incoming * normed, axis=-1, keepdims=True))


def project(left_side, matrix):
    return jnp.dot(left_side, matrix, preferred_element_type=jnp.float32).astype(jnp.bfloat16)


def project_back(left_side, matrix):
    return lax.dot_general(
        left_side, matrix, (((1,), (1,)), ((), ())), preferred_element_type=jnp.float32
    )


def split_heads(flat_rows, sequences):
    return flat_rows.reshape(sequences, -1, flat_rows.shape[1] // HEAD_DIM, HEAD_DIM)


def attend(query_rows, key_rows, matrices, sequences):
    query_normed, query_factor = normalize(query_rows)
    key_normed, key_factor = normalize(key_rows)
    query_low = query_normed.astype(jnp.bfloat16)
    key_low = key_normed.astype(jnp.bfloat16)
    query_vectors = project(query_low, matrices[0])
    key_vectors = project(key_low, matrices[1])
    value_vectors = project(key_low, matrices[2])
    scores = jnp.einsum(
        "sqhe,skhe->shqk",
        split_heads(query_vectors, sequences),
        split_heads(key_vectors, sequences),
        preferred_element_type=jnp.float32,
    ) * HEAD_DIM ** (-0.5)
    raised = jnp.exp(scores)
    attention = (raised / jnp.sum(raised, axis=-1, keepdims=True)).astype(jnp.bfloat16)
    context = jnp.einsum(
        "shqk,skhe->sqhe",
        attention,
        split_heads(value_vectors, sequences),
        preferred_element_type=jnp.float32,
    )
    context = context.astype(jnp.bfloat16).reshape(query_vectors.shape)
    return (
        query_normed,
        query_factor,
        key_normed,
        key_factor,
        query_low,
        key_low,
        query_vectors,
        key_vectors,
        value_vectors,
        attention,
        context,
    )


def attend_backward(query_rows, key_rows, grad_rows, matrices, sequences):
    (
        query_normed,
        query_factor,
        key_normed,
        key_factor,
        query_low,
        key_low,
        query_vectors,
        key_vectors,
        value_vectors,
        attention,
        context,
    ) = attend(query_rows, key_rows, matrices, sequences)
    grad_context = project(grad_rows, matrices[3])
    split_grad = split_heads(grad_context, sequences)
    grad_attention = jnp.einsum(
        "sqhe,skhe->shqk",
        split_grad,
        split_heads(value_vectors, sequences),
        preferred_element_type=jnp.float32,
    )
    grad_values = jnp.einsum(
        "shqk,sqhe->skhe", attention, split_grad, preferred_element_type=jnp.float32
    )
    grad_values = grad_values.astype(jnp.bfloat16).reshape(grad_context.shape)
    widened = attention.astype(jnp.float32)
    grad_scores = (
        widened
        * (grad_attention - jnp.sum(grad_attention * widened, axis=-1, keepdims=True))
        * HEAD_DIM ** (-0.5)
    ).astype(jnp.bfloat16)
    grad_queries = (
        jnp.einsum(
            "shqk,skhe->sqhe",
            grad_scores,
            split_heads(key_vectors, sequences),
            preferred_element_type=jnp.float32,
        )
        .astype(jnp.bfloat16)
        .reshape(grad_context.shape)
    )
    grad_keys = (
        jnp.einsum(
            "shqk,sqhe->skhe",
            grad_scores,
            split_heads(query_vectors, sequences),
            preferred_element_type=jnp.float32,
        )
        .astype(jnp.bfloat16)
        .reshape(grad_context.shape)
    )
    back_query = project_back(grad_queries, matrices[0])
    back_key = project_back(grad_keys, matrices[1]) + project_back(grad_values, matrices[2])
    head_terms = jnp.concatenate(
        [
            norm_back(query_normed, query_factor, back_query),
            norm_back(key_normed, key_factor, back_key),
        ],
        axis=0,
    )
    return (head_terms, (query_low, key_low, context, grad_queries, grad_keys, grad_values))


def collect(query_side, key_side):
    return (
        lax.all_gather(query_side, "mp", axis=1, tiled=True),
        lax.all_gather(key_side, "mp", axis=1, tiled=True),
    )


def head_sum(head_terms):
    return lax.psum_scatter(
        head_terms.astype(jnp.bfloat16), "mp", scatter_dimension=1, tiled=True
    ).astype(jnp.float32)


def hand_on(first_part, second_part, offset):
    return passed_along((first_part, second_part), "section", offset)


def store(stash_bank, update, position, active):
    current = lax.dynamic_index_in_dim(stash_bank, position, 0, keepdims=False)
    return lax.dynamic_update_index_in_dim(
        stash_bank, jnp.where(active, update, current), position, 0
    )


def per_device(enc_input, dec_input, cotangent, target_lengths, weights):
    section_count = lax.axis_size("section")
    section_index = lax.axis_index("section")
    decoder_side = section_index >= section_count // 2
    micro_count, sequences, seq_length, feature_part = enc_input.shape
    row_count = sequences * seq_length
    full_weights = lax.all_gather(weights, "dp", axis=2, tiled=True)
    matrices = full_weights[0]
    model_width = matrices.shape[1]
    column_count = matrices.shape[2]
    tick_count = section_count + micro_count - 1
    enc_rows = enc_input.reshape(micro_count, row_count, feature_part)
    dec_rows = dec_input.reshape(micro_count, row_count, feature_part)
    empty_bank = jnp.zeros((micro_count, row_count, feature_part), jnp.bfloat16)
    empty_stream = jnp.zeros((row_count, feature_part), jnp.bfloat16)
    tick_list = jnp.arange(tick_count, dtype=jnp.int32)

    def forward_step(state_now, tick_index):
        held_enc, held_dec, bank_query, bank_key = state_now
        position = tick_index - section_index
        active = (position >= 0) & (position < micro_count)
        position = jnp.clip(position, 0, micro_count - 1)
        starting = section_index == 0
        stream_enc = jnp.where(
            starting, lax.dynamic_index_in_dim(enc_rows, position, 0, keepdims=False), held_enc
        )
        stream_dec = jnp.where(
            starting, lax.dynamic_index_in_dim(dec_rows, position, 0, keepdims=False), held_dec
        )
        query_side = jnp.where(decoder_side, stream_dec, stream_enc)
        full_query, full_key = collect(query_side, stream_enc)
        bank_query = store(bank_query, query_side, position, active)
        bank_key = store(bank_key, stream_enc, position, active)

        def forward_compute(operands):
            return project_back(
                attend(operands[0], operands[1], matrices, sequences)[-1], matrices[3]
            )

        def forward_skipped(operands):
            return jnp.zeros((row_count, model_width), jnp.float32)

        partial_terms = lax.cond(active, forward_compute, forward_skipped, (full_query, full_key))
        summed = head_sum(partial_terms)
        updated_enc = jnp.where(
            decoder_side, stream_enc, (stream_enc.astype(jnp.float32) + summed).astype(jnp.bfloat16)
        )
        updated_dec = jnp.where(
            decoder_side, (stream_dec.astype(jnp.float32) + summed).astype(jnp.bfloat16), stream_dec
        )
        next_enc, next_dec = hand_on(updated_enc, updated_dec, 1)
        return ((next_enc, next_dec, bank_query, bank_key), None)

    forward_state, unused_out = lax.scan(
        forward_step, (empty_stream, empty_stream, empty_bank, empty_bank), tick_list
    )
    bank_query = forward_state[2]
    bank_key = forward_state[3]
    loss_scale = lax.rsqrt(jnp.float32(micro_count * sequences * lax.axis_size("dp") * seq_length))
    offsets = lax.broadcasted_iota(jnp.int32, (micro_count, sequences, seq_length), 2)
    live_rows = (offsets < target_lengths[:, :, None]).astype(jnp.float32)
    seed_grads = (cotangent.astype(jnp.float32) * live_rows[..., None] * loss_scale).astype(
        jnp.bfloat16
    )
    seed_grads = seed_grads.reshape(micro_count, row_count, feature_part)
    wide_bank = jnp.zeros((micro_count, row_count, model_width), jnp.bfloat16)
    narrow_bank = jnp.zeros((micro_count, row_count, column_count), jnp.bfloat16)
    start_banks = (
        wide_bank,
        wide_bank,
        wide_bank,
        narrow_bank,
        narrow_bank,
        narrow_bank,
        narrow_bank,
    )

    def backward_step(state_now, tick_index):
        held_enc, held_dec, stash_banks = state_now
        position = tick_index - (section_count - 1 - section_index)
        active = (position >= 0) & (position < micro_count)
        position = jnp.clip(position, 0, micro_count - 1)
        ending = section_index == section_count - 1
        grad_enc = jnp.where(ending, jnp.zeros_like(held_enc), held_enc)
        grad_dec = jnp.where(
            ending, lax.dynamic_index_in_dim(seed_grads, position, 0, keepdims=False), held_dec
        )
        grad_side = jnp.where(decoder_side, grad_dec, grad_enc)
        full_grad = lax.all_gather(grad_side, "mp", axis=1, tiled=True)
        kept_query = lax.dynamic_index_in_dim(bank_query, position, 0, keepdims=False)
        kept_key = lax.dynamic_index_in_dim(bank_key, position, 0, keepdims=False)
        full_query, full_key = collect(kept_query, kept_key)

        def backward_compute(operands):
            return attend_backward(operands[0], operands[1], operands[2], matrices, sequences)

        def backward_skipped(operands):
            wide_zero = jnp.zeros((row_count, model_width), jnp.bfloat16)
            narrow_zero = jnp.zeros((row_count, column_count), jnp.bfloat16)
            return (
                jnp.zeros((2 * row_count, model_width), jnp.float32),
                (wide_zero, wide_zero, narrow_zero, narrow_zero, narrow_zero, narrow_zero),
            )

        head_terms, pieces = lax.cond(
            active, backward_compute, backward_skipped, (full_query, full_key, full_grad)
        )
        summed = head_sum(head_terms)
        from_query = summed[:row_count]
        from_key = summed[row_count:]
        new_enc = (
            grad_enc.astype(jnp.float32) + from_key + jnp.where(decoder_side, 0.0, from_query)
        ).astype(jnp.bfloat16)
        new_dec = (grad_dec.astype(jnp.float32) + jnp.where(decoder_side, from_query, 0.0)).astype(
            jnp.bfloat16
        )
        stash_banks = tuple(
            (
                store(stored, fresh, position, active)
                for stored, fresh in zip(stash_banks, (full_grad,) + pieces)
            )
        )
        next_enc, next_dec = hand_on(new_enc, new_dec, -1)
        return ((next_enc, next_dec, stash_banks), None)

    backward_state, unused_grads = lax.scan(
        backward_step, (empty_stream, empty_stream, start_banks), tick_list
    )
    flattened = [stored.reshape(micro_count * row_count, -1) for stored in backward_state[2]]
    grad_all, query_all, key_all, context_all, gq_all, gk_all, gv_all = flattened
    factor_pairs = (
        (query_all, gq_all),
        (key_all, gk_all),
        (key_all, gv_all),
        (grad_all, context_all),
    )
    blocks = [
        lax.dot_general(
            left_side, right_side, (((0,), (0,)), ((), ())), preferred_element_type=jnp.float32
        )
        for left_side, right_side in factor_pairs
    ]
    owned_rows = lax.psum_scatter(
        jnp.concatenate(blocks, axis=1).astype(jnp.bfloat16), "dp", scatter_dimension=0, tiled=True
    ).astype(jnp.float32)
    return owned_rows.reshape(-1, 4, column_count).transpose(1, 0, 2)[None]


def solution(mesh):
    in_specs = (
        P(None, "dp", None, "mp"),
        P(None, "dp", None, "mp"),
        P(None, "dp", None, "mp"),
        P(None, "dp"),
        P("section", None, "dp", "mp"),
    )
    out_specs = P("section", None, "dp", "mp")
    return jax.shard_map(
        per_device, mesh=mesh, in_specs=in_specs, out_specs=out_specs, check_vma=False
    )
```

profile of v0, /device:TPU:1, one launch (start us, length us, event | category | flops | bytes accessed | tf_op | source)
XLA Modules:
  0.0 2431.7 jit_solution(14007081522104801920)
XLA Ops:
  9.0 332.2 %all-gather.8.cloned.1.call-done = bf16[1,4,4096,512]{3,2,1,0:T(8,128)(2,1)} async-done(((bf16[1,4,512,512]{3,2,1,0:T(8,128)(2,1)}), bf16[1,4,4096,512]{3,2,1,0:T(8,128)(2,1)}) %all-gather.8.cloned.1.call-update) | async-done | bytes 16777232 | tf_op jit(solution)/shard_map/all_gather | solution.py:174
  341.2 764.0 %while.45 = (s32[]{:T(128)}, bf16[16,1024]{1,0:T(8,128)(2,1)S(1)}, bf16[16,1024]{1,0:T(8,128)(2,1)S(1)}, bf16[4,16,1024]{2,1,0:T(8,128)(2,1)S(1)}, bf16[4,16,102...) while((s32[]{:T(128)}, bf16[16,1024]{1,0:T(8,128)(2,1)S(1)}, ...), condition=%wide.region_7.8_spmd, body=%wide.region_0.7_spmd.sunk | while | flops 270222912 | bytes 20059120 | solution.py:221
  343.3 7.4 all_gather.30
  351.6 6.9 all_gather.31
  358.5 12.6 conditional.4
  371.8 26.6 %reduce-scatter.6.cloned.1.call-done = bf16[16,1024]{1,0:T(8,128)(2,1)} async-done(((bf16[16,4096]{1,0:T(8,128)(2,1)}), bf16[16,1024]{1,0:T(8,128)(2,1)}) %reduce-scatter.6.cloned.1.call-update) | async-done | bytes 32784 | tf_op jit(solution)/shard_map/while/body/eval_jaxpr/reduce_scatter | solution.py:152
  408.7 9.0 all_gather.30
  418.5 6.9 all_gather.31
  425.4 12.6 conditional.4
  438.7 26.9 %reduce-scatter.6.cloned.1.call-done = bf16[16,1024]{1,0:T(8,128)(2,1)} async-done(((bf16[16,4096]{1,0:T(8,128)(2,1)}), bf16[16,1024]{1,0:T(8,128)(2,1)}) %reduce-scatter.6.cloned.1.call-update) | async-done | bytes 32784 | tf_op jit(solution)/shard_map/while/body/eval_jaxpr/reduce_scatter | solution.py:152
  475.9 9.0 all_gather.30
  485.7 6.9 all_gather.31
  492.6 12.6 conditional.4
  505.9 28.3 %reduce-scatter.6.cloned.1.call-done = bf16[16,1024]{1,0:T(8,128)(2,1)} async-done(((bf16[16,4096]{1,0:T(8,128)(2,1)}), bf16[16,1024]{1,0:T(8,128)(2,1)}) %reduce-scatter.6.cloned.1.call-update) | async-done | bytes 32784 | tf_op jit(solution)/shard_map/while/body/eval_jaxpr/reduce_scatter | solution.py:152
  544.5 9.0 all_gather.30
  554.3 6.9 all_gather.31
  561.2 12.6 conditional.4
  574.5 30.1 %reduce-scatter.6.cloned.1.call-done = bf16[16,1024]{1,0:T(8,128)(2,1)} async-done(((bf16[16,4096]{1,0:T(8,128)(2,1)}), bf16[16,1024]{1,0:T(8,128)(2,1)}) %reduce-scatter.6.cloned.1.call-update) | async-done | bytes 32784 | tf_op jit(solution)/shard_map/while/body/eval_jaxpr/reduce_scatter | solution.py:152
  614.8 9.0 all_gather.30
  624.7 6.9 all_gather.31
  632.3 43.9 %reduce-scatter.6.cloned.1.call-done = bf16[16,1024]{1,0:T(8,128)(2,1)} async-done(((bf16[16,4096]{1,0:T(8,128)(2,1)}), bf16[16,1024]{1,0:T(8,128)(2,1)}) %reduce-scatter.6.cloned.1.call-update) | async-done | bytes 32784 | tf_op jit(solution)/shard_map/while/body/eval_jaxpr/reduce_scatter | solution.py:152
  686.5 9.0 all_gather.30
  696.3 6.9 all_gather.31
  703.9 43.9 %reduce-scatter.6.cloned.1.call-done = bf16[16,1024]{1,0:T(8,128)(2,1)} async-done(((bf16[16,4096]{1,0:T(8,128)(2,1)}), bf16[16,1024]{1,0:T(8,128)(2,1)}) %reduce-scatter.6.cloned.1.call-update) | async-done | bytes 32784 | tf_op jit(solution)/shard_map/while/body/eval_jaxpr/reduce_scatter | solution.py:152
  758.1 9.0 all_gather.30
  768.0 6.9 all_gather.31
  775.6 43.9 %reduce-scatter.6.cloned.1.call-done = bf16[16,1024]{1,0:T(8,128)(2,1)} async-done(((bf16[16,4096]{1,0:T(8,128)(2,1)}), bf16[16,1024]{1,0:T(8,128)(2,1)}) %reduce-scatter.6.cloned.1.call-update) | async-done | bytes 32784 | tf_op jit(solution)/shard_map/while/body/eval_jaxpr/reduce_scatter | solution.py:152
  829.8 9.1 all_gather.30
  847.3 43.9 %reduce-scatter.6.cloned.1.call-done = bf16[16,1024]{1,0:T(8,128)(2,1)} async-done(((bf16[16,4096]{1,0:T(8,128)(2,1)}), bf16[16,1024]{1,0:T(8,128)(2,1)}) %reduce-scatter.6.cloned.1.call-update) | async-done | bytes 32784 | tf_op jit(solution)/shard_map/while/body/eval_jaxpr/reduce_scatter | solution.py:152
  901.5 9.0 all_gather.30
  918.9 41.9 %reduce-scatter.6.cloned.1.call-done = bf16[16,1024]{1,0:T(8,128)(2,1)} async-done(((bf16[16,4096]{1,0:T(8,128)(2,1)}), bf16[16,1024]{1,0:T(8,128)(2,1)}) %reduce-scatter.6.cloned.1.call-update) | async-done | bytes 32784 | tf_op jit(solution)/shard_map/while/body/eval_jaxpr/reduce_scatter | solution.py:152
  971.1 9.0 all_gather.30
  988.6 41.1 %reduce-scatter.6.cloned.1.call-done = bf16[16,1024]{1,0:T(8,128)(2,1)} async-done(((bf16[16,4096]{1,0:T(8,128)(2,1)}), bf16[16,1024]{1,0:T(8,128)(2,1)}) %reduce-scatter.6.cloned.1.call-update) | async-done | bytes 32784 | tf_op jit(solution)/shard_map/while/body/eval_jaxpr/reduce_scatter | solution.py:152
  1039.9 9.0 all_gather.30
  1057.4 39.7 %reduce-scatter.6.cloned.1.call-done = bf16[16,1024]{1,0:T(8,128)(2,1)} async-done(((bf16[16,4096]{1,0:T(8,128)(2,1)}), bf16[16,1024]{1,0:T(8,128)(2,1)}) %reduce-scatter.6.cloned.1.call-update) | async-done | bytes 32784 | tf_op jit(solution)/shard_map/while/body/eval_jaxpr/reduce_scatter | solution.py:152
  1105.5 971.7 %while.46 = (s32[]{:T(128)}, bf16[16,1024]{1,0:T(8,128)(2,1)S(1)}, bf16[16,1024]{1,0:T(8,128)(2,1)S(1)}, bf16[4,16,4096]{2,1,0:T(8,128)(2,1)S(1)}, bf16[4,16,409...) while((s32[]{:T(128)}, bf16[16,1024]{1,0:T(8,128)(2,1)S(1)}, ...), condition=%wide.region_18.19_spmd, body=%wide.region_8.18_spmd.sunk | while | flops 474587712 | bytes 39973692 | solution.py:293
  1106.8 9.0 all_gather.32
  1133.9 50.8 %reduce-scatter.8.cloned.1.call-done = bf16[32,1024]{1,0:T(8,128)(2,1)} async-done(((bf16[32,4096]{1,0:T(8,128)(2,1)}), bf16[32,1024]{1,0:T(8,128)(2,1)}) %reduce-scatter.8.cloned.1.call-update) | async-done | bytes 65552 | tf_op jit(solution)/shard_map/while/body/eval_jaxpr/reduce_scatter | solution.py:152
  1193.5 8.6 all_gather.32
  1220.2 53.8 %reduce-scatter.8.cloned.1.call-done = bf16[32,1024]{1,0:T(8,128)(2,1)} async-done(((bf16[32,4096]{1,0:T(8,128)(2,1)}), bf16[32,1024]{1,0:T(8,128)(2,1)}) %reduce-scatter.8.cloned.1.call-update) | async-done | bytes 65552 | tf_op jit(solution)/shard_map/while/body/eval_jaxpr/reduce_scatter | solution.py:152
  1282.7 8.6 all_gather.32
  1309.4 54.5 %reduce-scatter.8.cloned.1.call-done = bf16[32,1024]{1,0:T(8,128)(2,1)} async-done(((bf16[32,4096]{1,0:T(8,128)(2,1)}), bf16[32,1024]{1,0:T(8,128)(2,1)}) %reduce-scatter.8.cloned.1.call-update) | async-done | bytes 65552 | tf_op jit(solution)/shard_map/while/body/eval_jaxpr/reduce_scatter | solution.py:152
  1372.7 8.6 all_gather.32
  1399.4 54.6 %reduce-scatter.8.cloned.1.call-done = bf16[32,1024]{1,0:T(8,128)(2,1)} async-done(((bf16[32,4096]{1,0:T(8,128)(2,1)}), bf16[32,1024]{1,0:T(8,128)(2,1)}) %reduce-scatter.8.cloned.1.call-update) | async-done | bytes 65552 | tf_op jit(solution)/shard_map/while/body/eval_jaxpr/reduce_scatter | solution.py:152
  1462.8 8.6 all_gather.32
  1489.5 54.5 %reduce-scatter.8.cloned.1.call-done = bf16[32,1024]{1,0:T(8,128)(2,1)} async-done(((bf16[32,4096]{1,0:T(8,128)(2,1)}), bf16[32,1024]{1,0:T(8,128)(2,1)}) %reduce-scatter.8.cloned.1.call-update) | async-done | bytes 65552 | tf_op jit(solution)/shard_map/while/body/eval_jaxpr/reduce_scatter | solution.py:152
  1552.8 8.6 all_gather.32
  1579.5 54.5 %reduce-scatter.8.cloned.1.call-done = bf16[32,1024]{1,0:T(8,128)(2,1)} async-done(((bf16[32,4096]{1,0:T(8,128)(2,1)}), bf16[32,1024]{1,0:T(8,128)(2,1)}) %reduce-scatter.8.cloned.1.call-update) | async-done | bytes 65552 | tf_op jit(solution)/shard_map/while/body/eval_jaxpr/reduce_scatter | solution.py:152
  1642.8 8.7 all_gather.32
  1669.5 54.5 %reduce-scatter.8.cloned.1.call-done = bf16[32,1024]{1,0:T(8,128)(2,1)} async-done(((bf16[32,4096]{1,0:T(8,128)(2,1)}), bf16[32,1024]{1,0:T(8,128)(2,1)}) %reduce-scatter.8.cloned.1.call-update) | async-done | bytes 65552 | tf_op jit(solution)/shard_map/while/body/eval_jaxpr/reduce_scatter | solution.py:152
  1732.7 8.6 all_gather.32
  1755.2 26.3 %conditional.5 = (bf16[32,4096]{1,0:T(8,128)(2,1)S(1)}, bf16[16,4096]{1,0:T(8,128)(2,1)}, bf16[16,4096]{1,0:T(8,128)(2,1)}, bf16[16,512]{1,0:T(8,128)(2,1)S(1)},...) conditional(s32[]{:T(128)} %convert_element_type.337, () %tuple.87, ...), branch_computations={%region_9.9_spmd, %region_10.16_spmd} | conditional | flops 474096192 | bytes 34140472 | solution.py:272
  1784.2 28.7 %reduce-scatter.8.cloned.1.call-done = bf16[32,1024]{1,0:T(8,128)(2,1)} async-done(((bf16[32,4096]{1,0:T(8,128)(2,1)}), bf16[32,1024]{1,0:T(8,128)(2,1)}) %reduce-scatter.8.cloned.1.call-update) | async-done | bytes 65552 | tf_op jit(solution)/shard_map/while/body/eval_jaxpr/reduce_scatter | solution.py:152
  1821.7 8.6 all_gather.32
  1844.2 26.3 %conditional.5 = (bf16[32,4096]{1,0:T(8,128)(2,1)S(1)}, bf16[16,4096]{1,0:T(8,128)(2,1)}, bf16[16,4096]{1,0:T(8,128)(2,1)}, bf16[16,512]{1,0:T(8,128)(2,1)S(1)},...) conditional(s32[]{:T(128)} %convert_element_type.337, () %tuple.87, ...), branch_computations={%region_9.9_spmd, %region_10.16_spmd} | conditional | flops 474096192 | bytes 34140472 | solution.py:272
  1873.2 26.5 %reduce-scatter.8.cloned.1.call-done = bf16[32,1024]{1,0:T(8,128)(2,1)} async-done(((bf16[32,4096]{1,0:T(8,128)(2,1)}), bf16[32,1024]{1,0:T(8,128)(2,1)}) %reduce-scatter.8.cloned.1.call-update) | async-done | bytes 65552 | tf_op jit(solution)/shard_map/while/body/eval_jaxpr/reduce_scatter | solution.py:152
  1908.5 8.6 all_gather.32
  1930.9 26.3 %conditional.5 = (bf16[32,4096]{1,0:T(8,128)(2,1)S(1)}, bf16[16,4096]{1,0:T(8,128)(2,1)}, bf16[16,4096]{1,0:T(8,128)(2,1)}, bf16[16,512]{1,0:T(8,128)(2,1)S(1)},...) conditional(s32[]{:T(128)} %convert_element_type.337, () %tuple.87, ...), branch_computations={%region_9.9_spmd, %region_10.16_spmd} | conditional | flops 474096192 | bytes 34140472 | solution.py:272
  1960.0 25.5 %reduce-scatter.8.cloned.1.call-done = bf16[32,1024]{1,0:T(8,128)(2,1)} async-done(((bf16[32,4096]{1,0:T(8,128)(2,1)}), bf16[32,1024]{1,0:T(8,128)(2,1)}) %reduce-scatter.8.cloned.1.call-update) | async-done | bytes 65552 | tf_op jit(solution)/shard_map/while/body/eval_jaxpr/reduce_scatter | solution.py:152
  1994.2 8.6 all_gather.32
  2016.7 26.3 %conditional.5 = (bf16[32,4096]{1,0:T(8,128)(2,1)S(1)}, bf16[16,4096]{1,0:T(8,128)(2,1)}, bf16[16,4096]{1,0:T(8,128)(2,1)}, bf16[16,512]{1,0:T(8,128)(2,1)S(1)},...) conditional(s32[]{:T(128)} %convert_element_type.337, () %tuple.87, ...), branch_computations={%region_9.9_spmd, %region_10.16_spmd} | conditional | flops 474096192 | bytes 34140472 | solution.py:272
  2045.7 24.0 reduce-scatter.8.cloned.1.call-done
  2082.4 7.6 pad_maximum_fusion.1
  2090.0 330.4 %reduce-scatter.4.cloned.1.call-done = bf16[512,2048]{0,1:T(8,128)(2,1)} async-done(((bf16[4096,2048]{0,1:T(8,128)(2,1)}), bf16[512,2048]{0,1:T(8,128)(2,1)}) %reduce-scatter.4.cloned.1.call-update) | async-done | bytes 2097168 | tf_op jit(solution)/shard_map/reduce_scatter | solution.py:310
  (719 shorter events, 618.5 us)
Async XLA Ops:
  6.5 334.6 %all-gather.8.cloned.1.call-start = ((), (), s32[]{:S(2)}) async-start(), calls=%async_computation.3 | async-start | bytes 18874368 | tf_op jit(solution)/shard_map/all_gather | solution.py:174
  341.2 57.2 %reduce-scatter.6.cloned.1.call-start = ((), (), s32[]{:S(2)}) async-start(), calls=%async_computation.5 | async-start | bytes 163840 | tf_op jit(solution)/shard_map/while/body/eval_jaxpr/reduce_scatter | solution.py:152
  399.2 6.4 collective-permute-start
  402.4 4.2 collective-permute-start.1
  406.6 59.0 %reduce-scatter.6.cloned.1.call-start = ((), (), s32[]{:S(2)}) async-start(), calls=%async_computation.5 | async-start | bytes 163840 | tf_op jit(solution)/shard_map/while/body/eval_jaxpr/reduce_scatter | solution.py:152
  466.4 6.4 collective-permute-start
  469.6 4.2 collective-permute-start.1
  473.8 60.4 %reduce-scatter.6.cloned.1.call-start = ((), (), s32[]{:S(2)}) async-start(), calls=%async_computation.5 | async-start | bytes 163840 | tf_op jit(solution)/shard_map/while/body/eval_jaxpr/reduce_scatter | solution.py:152
  535.0 6.4 collective-permute-start
  538.2 4.2 collective-permute-start.1
  542.4 62.2 %reduce-scatter.6.cloned.1.call-start = ((), (), s32[]{:S(2)}) async-start(), calls=%async_computation.5 | async-start | bytes 163840 | tf_op jit(solution)/shard_map/while/body/eval_jaxpr/reduce_scatter | solution.py:152
  605.4 6.4 collective-permute-start
  612.8 63.5 %reduce-scatter.6.cloned.1.call-start = ((), (), s32[]{:S(2)}) async-start(), calls=%async_computation.5 | async-start | bytes 163840 | tf_op jit(solution)/shard_map/while/body/eval_jaxpr/reduce_scatter | solution.py:152
  677.0 6.4 collective-permute-start
  680.2 4.2 collective-permute-start.1
  684.4 63.5 %reduce-scatter.6.cloned.1.call-start = ((), (), s32[]{:S(2)}) async-start(), calls=%async_computation.5 | async-start | bytes 163840 | tf_op jit(solution)/shard_map/while/body/eval_jaxpr/reduce_scatter | solution.py:152
  748.7 6.4 collective-permute-start
  756.1 63.5 %reduce-scatter.6.cloned.1.call-start = ((), (), s32[]{:S(2)}) async-start(), calls=%async_computation.5 | async-start | bytes 163840 | tf_op jit(solution)/shard_map/while/body/eval_jaxpr/reduce_scatter | solution.py:152
  820.3 6.4 collective-permute-start
  827.7 63.5 %reduce-scatter.6.cloned.1.call-start = ((), (), s32[]{:S(2)}) async-start(), calls=%async_computation.5 | async-start | bytes 163840 | tf_op jit(solution)/shard_map/while/body/eval_jaxpr/reduce_scatter | solution.py:152
  892.0 6.4 collective-permute-start
  895.2 4.2 collective-permute-start.1
  899.4 61.5 %reduce-scatter.6.cloned.1.call-start = ((), (), s32[]{:S(2)}) async-start(), calls=%async_computation.5 | async-start | bytes 163840 | tf_op jit(solution)/shard_map/while/body/eval_jaxpr/reduce_scatter | solution.py:152
  961.6 6.4 collective-permute-start
  964.8 4.2 collective-permute-start.1
  969.0 60.6 %reduce-scatter.6.cloned.1.call-start = ((), (), s32[]{:S(2)}) async-start(), calls=%async_computation.5 | async-start | bytes 163840 | tf_op jit(solution)/shard_map/while/body/eval_jaxpr/reduce_scatter | solution.py:152
  1030.5 6.4 collective-permute-start
  1037.8 59.2 %reduce-scatter.6.cloned.1.call-start = ((), (), s32[]{:S(2)}) async-start(), calls=%async_computation.5 | async-start | bytes 163840 | tf_op jit(solution)/shard_map/while/body/eval_jaxpr/reduce_scatter | solution.py:152
  1097.9 6.4 collective-permute-start
  1101.1 4.2 collective-permute-start.1
  1105.5 79.3 %reduce-scatter.8.cloned.1.call-start = ((), (), s32[]{:S(2)}) async-start(), calls=%async_computation.6 | async-start | bytes 327680 | tf_op jit(solution)/shard_map/while/body/eval_jaxpr/reduce_scatter | solution.py:152
  1185.6 4.7 collective-permute-start.2
  1186.9 5.3 collective-permute-start.3
  1192.2 81.7 %reduce-scatter.8.cloned.1.call-start = ((), (), s32[]{:S(2)}) async-start(), calls=%async_computation.6 | async-start | bytes 327680 | tf_op jit(solution)/shard_map/while/body/eval_jaxpr/reduce_scatter | solution.py:152
  1274.8 4.7 collective-permute-start.2
  1276.2 5.3 collective-permute-start.3
  1281.4 82.5 %reduce-scatter.8.cloned.1.call-start = ((), (), s32[]{:S(2)}) async-start(), calls=%async_computation.6 | async-start | bytes 327680 | tf_op jit(solution)/shard_map/while/body/eval_jaxpr/reduce_scatter | solution.py:152
  1364.8 4.7 collective-permute-start.2
  1366.1 5.3 collective-permute-start.3
  1371.4 82.5 %reduce-scatter.8.cloned.1.call-start = ((), (), s32[]{:S(2)}) async-start(), calls=%async_computation.6 | async-start | bytes 327680 | tf_op jit(solution)/shard_map/while/body/eval_jaxpr/reduce_scatter | solution.py:152
  1454.9 4.7 collective-permute-start.2
  1456.2 5.3 collective-permute-start.3
  1461.5 82.5 %reduce-scatter.8.cloned.1.call-start = ((), (), s32[]{:S(2)}) async-start(), calls=%async_computation.6 | async-start | bytes 327680 | tf_op jit(solution)/shard_map/while/body/eval_jaxpr/reduce_scatter | solution.py:152
  1544.9 4.7 collective-permute-start.2
  1546.2 5.3 collective-permute-start.3
  1551.5 82.5 %reduce-scatter.8.cloned.1.call-start = ((), (), s32[]{:S(2)}) async-start(), calls=%async_computation.6 | async-start | bytes 327680 | tf_op jit(solution)/shard_map/while/body/eval_jaxpr/reduce_scatter | solution.py:152
  1634.9 4.7 collective-permute-start.2
  1636.2 5.3 collective-permute-start.3
  1641.5 82.5 %reduce-scatter.8.cloned.1.call-start = ((), (), s32[]{:S(2)}) async-start(), calls=%async_computation.6 | async-start | bytes 327680 | tf_op jit(solution)/shard_map/while/body/eval_jaxpr/reduce_scatter | solution.py:152
  1724.8 4.7 collective-permute-start.2
  1726.1 5.3 collective-permute-start.3
  1731.4 81.5 %reduce-scatter.8.cloned.1.call-start = ((), (), s32[]{:S(2)}) async-start(), calls=%async_computation.6 | async-start | bytes 327680 | tf_op jit(solution)/shard_map/while/body/eval_jaxpr/reduce_scatter | solution.py:152
  1813.8 4.7 collective-permute-start.2
  1815.1 5.3 collective-permute-start.3
  1820.4 79.3 %reduce-scatter.8.cloned.1.call-start = ((), (), s32[]{:S(2)}) async-start(), calls=%async_computation.6 | async-start | bytes 327680 | tf_op jit(solution)/shard_map/while/body/eval_jaxpr/reduce_scatter | solution.py:152
  1900.6 4.7 collective-permute-start.2
  1901.9 5.3 collective-permute-start.3
  1907.2 78.3 %reduce-scatter.8.cloned.1.call-start = ((), (), s32[]{:S(2)}) async-start(), calls=%async_computation.6 | async-start | bytes 327680 | tf_op jit(solution)/shard_map/while/body/eval_jaxpr/reduce_scatter | solution.py:152
  1986.3 4.7 collective-permute-start.2
  1987.6 5.3 collective-permute-start.3
  1992.9 76.8 %reduce-scatter.8.cloned.1.call-start = ((), (), s32[]{:S(2)}) async-start(), calls=%async_computation.6 | async-start | bytes 327680 | tf_op jit(solution)/shard_map/while/body/eval_jaxpr/reduce_scatter | solution.py:152
  2070.6 4.7 collective-permute-start.2
  2071.9 5.3 collective-permute-start.3
  2077.2 343.2 %reduce-scatter.4.cloned.1.call-start = ((), (), s32[]{:S(2)}) async-start(), calls=%async_computation.4 | async-start | bytes 18874368 | tf_op jit(solution)/shard_map/reduce_scatter | solution.py:310
  (26 other events, 31.8 us)
Sparse Core Ops, SparseCore 0:
  9.1 331.9 all-gather.7
  371.9 26.4 reduce-scatter.5
  438.9 26.7 reduce-scatter.5
  506.0 28.1 reduce-scatter.5
  574.6 29.9 reduce-scatter.5
  632.4 43.7 reduce-scatter.5
  704.1 43.7 reduce-scatter.5
  775.7 43.7 reduce-scatter.5
  847.4 43.7 reduce-scatter.5
  919.0 41.7 reduce-scatter.5
  988.7 40.9 reduce-scatter.5
  1057.5 39.5 reduce-scatter.5
  1133.7 50.9 reduce-scatter.7
  1220.0 53.9 reduce-scatter.7
  1309.2 54.6 reduce-scatter.7
  1399.2 54.7 reduce-scatter.7
  1489.3 54.6 reduce-scatter.7
  1579.3 54.6 reduce-scatter.7
  1669.3 54.6 reduce-scatter.7
  1782.4 30.4 reduce-scatter.7
  1871.3 28.2 reduce-scatter.7
  1958.1 27.2 reduce-scatter.7
  2043.9 25.8 reduce-scatter.7
  2090.1 330.2 reduce-scatter.3
where the time goes:
time: 2440 us; the launch traced here: 2430 us
  waiting for transfers between devices  1610 us (66%)
  blocking collectives  422 us (17%)
  matrix products  146 us (6%)
  starting transfers between devices  98.5 us (4%)
  local copies, waits for them, and re-layouts  63.7 us (3%)
  other arithmetic  63.1 us (3%)
    reduce_scatter x22, waiting for transfers between devices, head_sum(): lax.psum_scatter(head_terms.astype(jnp.bfloat16), 'mp', scatter_dimension...  892 us
    all_gather x1, waiting for transfers between devices, per_device(): full_weights = lax.all_gather(weights, 'dp', axis=2, tiled=True)  332 us
    reduce_scatter x1, waiting for transfers between devices, per_device(): lax.psum_scatter(jnp.concatenate(blocks, axis=1).astype(jnp.bfloat16), 'd...  330 us
    all_gather x22, blocking collectives, collect(): lax.all_gather(key_side, 'mp', axis=1, tiled=True)  174 us
    all_gather x22, blocking collectives, collect(): lax.all_gather(query_side, 'mp', axis=1, tiled=True)  152 us
    ppermute x44, starting transfers between devices, passed_along(): return lax.ppermute(value, axis, pairs)  98.4 us
    all_gather x11, blocking collectives, backward_step(): full_grad = lax.all_gather(grad_side, 'mp', axis=1, tiled=True)  95.5 us
    dot_general x28, matrix products, project(): jnp.dot(left_side, matrix, preferred_element_type=jnp.float32)  80.9 us
  transfers between devices with their start and end apart: 68, of which 57 were waited for; matrix products, arithmetic and copies ran while one was open for 1% of the time, Pallas kernels for 0%

commit v1 on v0

v1 whole, which is shorter than its diff:
```python
import functools

import jax
import jax.numpy as jnp
from jax import lax
from jax.experimental import pallas as pl
from jax.experimental.pallas import tpu as pltpu
from jax.sharding import PartitionSpec as P

HEAD_DIM = 256
EPSILON = 1e-06
MICRO = 4
BF = jnp.bfloat16
F32 = jnp.float32
MESH = pl.DeviceIdType.MESH
NT = (((1,), (1,)), ((), ()))
NN = (((1,), (0,)), ((), ()))
TN = (((0,), (0,)), ((), ()))


def dot(a, b, dims=NN):
    return lax.dot_general(a, b, dims, preferred_element_type=F32)


def layer_kernel(
    width,
    start_ref, weights_ref, out_ref,
    w, xs, part, qrecv, qs, ks, vs, ps, rr, cs, oown, ost, orecv, xn,
    dpart, drecv, dd, cc, uown, ust, urecv, wown, wst, wrecv, gn, gein, geout, ob,
    g_ss, g_rs, i_ss, x_rs, f_ss, q_ss, q_rs, c_ss, c_rs, o_ss, o_rs, n_ss,
    d_ss, d_rs, dd_ss, dd_rs, cc_ss, cc_rs, u_ss, u_rs, w_ss, w_rs, e_ss, e_rs, gn_ss,
    b_ss, b_rs,
):
    s = lax.axis_index("section")
    d = lax.axis_index("dp")
    p = lax.axis_index("mp")
    t = d // 2
    c = lax.rem(p, 2)
    j = 2 * (p // 2) + lax.rem(d, 2)
    decoder = s >= 4
    sel = jnp.where(decoder, 1, 0)
    starts = (s == 0) | (s == 4) | (s == 7)
    start_stream = jnp.where(s == 0, 0, jnp.where(s == 4, 1, 2))

    def place(tt, jj, ccc):
        return 2 * tt + lax.rem(jj, 2), 2 * (jj // 2) + ccc

    def member(k):
        return place(t, lax.rem(j + k, 4), c)

    gather_to = [place(k, p, d // 4) for k in range(4)]
    owner = [(4 * c + b, j) for b in range(4)]
    start_to = [place(t, jnp.int32(k), p // 2) for k in range(4)]
    start_from = [(2 * t + a, 2 * c + e) for a in range(2) for e in range(2)]

    def same(dev):
        return (dev[0] == d) & (dev[1] == p)

    def remote(src, dst, ss, rs, dev, sec=None):
        ids = {"dp": dev[0], "mp": dev[1]}
        if sec is not None:
            ids["section"] = sec
        return pltpu.make_async_remote_copy(
            src_ref=src, dst_ref=dst, send_sem=ss, recv_sem=rs, device_id=ids, device_id_type=MESH
        )

    def arrived(ref, sem):
        pltpu.make_async_copy(ref, ref, sem).wait()

    def send_any(src, dst, ss, rs, dev):
        here = same(dev)

        @pl.when(here)
        def _():
            pltpu.make_async_copy(src, dst, rs).start()

        @pl.when(jnp.logical_not(here))
        def _():
            remote(src, dst, ss, rs, dev).start()

    def sent_any(src, ss, dev):
        @pl.when(jnp.logical_not(same(dev)))
        def _():
            arrived(src, ss)

    bar = pltpu.get_barrier_semaphore()

    def greet(dev, sec=None):
        ids = {"dp": dev[0], "mp": dev[1]}
        if sec is not None:
            ids["section"] = sec
        pl.semaphore_signal(bar, inc=1, device_id=ids, device_id_type=MESH)

    greet((d, p + 1 - 2 * c))
    for k in range(1, 4):
        greet(member(k))

    @pl.when(s > 0)
    def _():
        for k in range(4):
            greet(member(k), s - 1)

    @pl.when(s < 7)
    def _():
        for k in range(4):
            greet(member(k), s + 1)

    for dev in gather_to + owner:
        @pl.when(jnp.logical_not(same(dev)))
        def _(dev=dev):
            greet(dev)

    @pl.when(starts)
    def _():
        for dev in start_from:
            @pl.when(jnp.logical_not(same(dev)))
            def _(dev=dev):
                greet(dev)

    own_shard = sum(jnp.where(same(dev), 1, 0) for dev in gather_to)
    own_start = sum(jnp.where(same(dev), 1, 0) for dev in start_to)
    count = 4 + jnp.where(s > 0, 4, 0) + jnp.where(s < 7, 4, 0) + 8 - 2 * own_shard
    count = count + jnp.where(starts, 4 - own_start, 0)
    pl.semaphore_wait(bar, count)

    @pl.when(starts)
    def _():
        for m in range(MICRO):
            for k in range(4):
                send_any(
                    start_ref.at[m],
                    xs.at[start_stream, m, pl.ds(2 * lax.rem(p, 2), 2), lax.rem(d, 2)],
                    i_ss.at[m, k], x_rs.at[start_stream, m], start_to[k],
                )

    for mat in range(4):
        for k in range(4):
            send_any(
                weights_ref.at[mat], w.at[mat, lax.rem(d, 4)], g_ss.at[mat, k], g_rs.at[mat],
                gather_to[k],
            )
    for mat in range(4):
        arrived(w.at[mat], g_rs.at[mat])

    def rows(value):
        return value.reshape(32, 512)

    def attend(m):
        arrived(xs.at[0, m], x_rs.at[0, m])

        @pl.when(decoder)
        def _():
            @pl.when(s < 7)
            def _():
                remote(
                    xs.at[0, m], xs.at[0, m], f_ss.at[m], x_rs.at[0, m], (d, p), s + 1
                ).start()

            arrived(xs.at[1, m], x_rs.at[1, m])

        sums = [None, None, None]
        squares = [None, None]
        for b in range(4):
            query = rows(xs[sel, m, b])
            key = rows(xs[0, m, b])
            for i, left in enumerate((query, key, key)):
                term = dot(left, w[i, b])
                sums[i] = term if b == 0 else sums[i] + term
            for i, left in enumerate((query, key)):
                wide = left.astype(F32)
                term = jnp.sum(wide * wide, axis=-1, keepdims=True)
                squares[i] = term if b == 0 else squares[i] + term
        for i in range(3):
            part[m, :, :, i * 512:(i + 1) * 512] = sums[i].reshape(2, 16, 512)
        for i in range(2):
            part[m, :, :, 1536 + i * 128:1664 + i * 128] = jnp.broadcast_to(
                squares[i], (32, 128)
            ).reshape(2, 16, 128)
        other = (d, p + 1 - 2 * c)
        remote(part.at[m, 1 - c], qrecv.at[m], q_ss.at[m], q_rs.at[m], other).start()
        arrived(qrecv.at[m], q_rs.at[m])
        total = part[m, c] + qrecv[m]
        factor_q = lax.rsqrt(total[:, 1536:1537] * (1.0 / width) + EPSILON)
        factor_k = lax.rsqrt(total[:, 1664:1665] * (1.0 / width) + EPSILON)
        rr[m, 0] = jnp.broadcast_to(factor_q, (16, 128))
        rr[m, 1] = jnp.broadcast_to(factor_k, (16, 128))
        query = (total[:, :512] * factor_q).astype(BF)
        key = (total[:, 512:1024] * factor_k).astype(BF)
        value = (total[:, 1024:1536] * factor_k).astype(BF)
        qs[m] = query
        ks[m] = key
        vs[m] = value
        contexts = []
        for h in range(2):
            cols = slice(h * HEAD_DIM, (h + 1) * HEAD_DIM)
            raised = jnp.exp(dot(query[:, cols], key[:, cols], NT) * HEAD_DIM ** (-0.5))
            weight = (raised / jnp.sum(raised, axis=-1, keepdims=True)).astype(BF)
            ps[m, h] = weight.astype(F32)
            contexts.append(dot(weight, value[:, cols]).astype(BF))
        cs[m, c] = jnp.concatenate(contexts, axis=1)
        remote(cs.at[m, c], cs.at[m, c], c_ss.at[m], c_rs.at[m], other).start()
        arrived(cs.at[m, c], c_rs.at[m])

        @pl.when(s < 7)
        def _():
            context = rows(cs[m])
            for k in (1, 2, 3, 0):
                term = dot(context, w[3, lax.rem(j + k, 4)], NT)
                if k == 0:
                    oown[m] = term
                else:
                    ost[m, k - 1] = term.astype(BF)
                    remote(
                        ost.at[m, k - 1], orecv.at[m, k - 1], o_ss.at[m, k - 1], o_rs.at[m],
                        member(k),
                    ).start()

    def advance(m):
        arrived(orecv.at[m], o_rs.at[m])
        total = rows(xs[sel, m, j]).astype(F32) + oown[m]
        for k in range(3):
            total = total + orecv[m, k].astype(F32)
        xn[m] = total.astype(BF).reshape(2, 16, 512)
        for k in range(4):
            remote(
                xn.at[m], xs.at[sel, m, j], n_ss.at[m, k], x_rs.at[sel, m], member(k), s + 1
            ).start()

    def forward_step(i, carry):
        @pl.when(i < MICRO)
        def _():
            attend(i)

        @pl.when((i > 0) & (s < 7))
        def _():
            advance(i - 1)

        return carry

    lax.fori_loop(0, MICRO + 1, forward_step, 0)

    def to_owners(src_of, slot):
        for b in range(4):
            send_any(src_of(b), ob.at[slot, :, t], b_ss.at[slot, b], b_rs.at[slot], owner[b])

    def owners_sent(src_of, slot):
        for b in range(4):
            sent_any(src_of(b), b_ss.at[slot, b], owner[b])

    to_owners(lambda b: xs.at[sel, :, b], 0)

    @pl.when(decoder)
    def _():
        to_owners(lambda b: xs.at[0, :, b], 1)

    to_owners(lambda b: cs, 3)

    def attend_back(m):
        arrived(xs.at[2, m], x_rs.at[2, m])
        total = None
        for b in range(4):
            term = dot(rows(xs[2, m, b]), w[3, b])
            total = term if b == 0 else total + term
        dpart[m] = total.reshape(2, 16, 512)
        other = (d, p + 1 - 2 * c)
        remote(dpart.at[m, 1 - c], drecv.at[m], d_ss.at[m], d_rs.at[m], other).start()
        arrived(drecv.at[m], d_rs.at[m])
        grad = (dpart[m, c] + drecv[m]).astype(BF)
        query, key, value = qs[m], ks[m], vs[m]
        pieces = [[], [], []]
        for h in range(2):
            cols = slice(h * HEAD_DIM, (h + 1) * HEAD_DIM)
            weight = ps[m, h]
            grad_weight = dot(grad[:, cols], value[:, cols], NT)
            pieces[2].append(dot(weight.astype(BF), grad[:, cols], TN))
            inner = jnp.sum(grad_weight * weight, axis=-1, keepdims=True)
            scores = (weight * (grad_weight - inner) * HEAD_DIM ** (-0.5)).astype(BF)
            pieces[0].append(dot(scores, key[:, cols]))
            pieces[1].append(dot(scores, query[:, cols], TN))
        grads = [jnp.concatenate(piece, axis=1) for piece in pieces]
        factors = [rr[m, 0][:, :1], rr[m, 1][:, :1], rr[m, 1][:, :1]]
        means = [
            jnp.sum(g * v.astype(F32), axis=-1, keepdims=True) * (1.0 / width)
            for g, v in zip(grads, (query, key, value))
        ]
        for i in range(3):
            dd[m, i, c] = (grads[i] * factors[i]).astype(BF)
        cc[m, 0, c] = jnp.broadcast_to(means[0] * factors[0] * factors[0], (16, 128))
        cc[m, 1, c] = jnp.broadcast_to((means[1] + means[2]) * factors[1] * factors[1], (16, 128))
        remote(dd.at[m, :, c], dd.at[m, :, c], dd_ss.at[m], dd_rs.at[m], other).start()
        remote(cc.at[m, :, c], cc.at[m, :, c], cc_ss.at[m], cc_rs.at[m], other).start()
        arrived(dd.at[m, :, c], dd_rs.at[m])
        arrived(cc.at[m, :, c], cc_rs.at[m])

        def spread(pairs, stream, kinds, own, stage, recv, ss, rs):
            lefts = [rows(dd[m, i]) for i in pairs]
            shift = sum(cc[m, i].reshape(32, 128)[:, :1] for i in kinds)
            for k in (1, 2, 3, 0):
                block = lax.rem(j + k, 4)
                term = -rows(xs[stream, m, block]).astype(F32) * shift
                for i, left in zip(pairs, lefts):
                    term = term + dot(left, w[i, block], NT)
                if k == 0:
                    own[m] = term
                else:
                    stage[m, k - 1] = term.astype(BF)
                    remote(
                        stage.at[m, k - 1], recv.at[m, k - 1], ss.at[m, k - 1], rs.at[m], member(k)
                    ).start()

        @pl.when((s > 0) & (s < 4))
        def _():
            spread((0, 1, 2), 0, (0, 1), uown, ust, urecv, u_ss, u_rs)

        @pl.when(s > 4)
        def _():
            spread((0,), 1, (0,), uown, ust, urecv, u_ss, u_rs)

        @pl.when(s >= 4)
        def _():
            spread((1, 2), 0, (1,), wown, wst, wrecv, w_ss, w_rs)

    def hand_back(m):
        for k in range(4):
            remote(
                gn.at[m], xs.at[2, m, j], gn_ss.at[m, k], x_rs.at[2, m], member(k), s - 1
            ).start()

    def advance_back(m):
        @pl.when(s != 4)
        def _():
            arrived(urecv.at[m], u_rs.at[m])
            total = rows(xs[2, m, j]).astype(F32) + uown[m]
            for k in range(3):
                total = total + urecv[m, k].astype(F32)
            gn[m] = total.astype(BF).reshape(2, 16, 512)
            hand_back(m)

        @pl.when(s >= 4)
        def _():
            arrived(wrecv.at[m], w_rs.at[m])
            total = wown[m]
            for k in range(3):
                total = total + wrecv[m, k].astype(F32)
            geout[m] = total.astype(BF).reshape(2, 16, 512)

            @pl.when(s < 7)
            def _():
                arrived(gein.at[m], e_rs.at[m])
                geout[m] = (total + rows(gein[m]).astype(F32)).astype(BF).reshape(2, 16, 512)

            @pl.when(s > 4)
            def _():
                remote(geout.at[m], gein.at[m], e_ss.at[m], e_rs.at[m], (d, p), s - 1).start()

            @pl.when(s == 4)
            def _():
                gn[m] = geout[m]
                hand_back(m)

    def backward_step(i, carry):
        @pl.when(i < MICRO)
        def _():
            attend_back(i)

        @pl.when((i > 0) & (s > 0))
        def _():
            advance_back(i - 1)

        return carry

    lax.fori_loop(0, MICRO + 1, backward_step, 0)

    to_owners(lambda b: xs.at[2, :, b], 2)
    for i in range(3):
        to_owners(lambda b: dd.at[:, i], 4 + i)

    key_slot = jnp.where(decoder, 1, 0)
    arrived(ob.at[3], b_rs.at[3])
    arrived(ob.at[2], b_rs.at[2])
    out_ref[3] = dot(ob[2].reshape(512, 512), ob[3].reshape(512, 512), TN)
    arrived(ob.at[0], b_rs.at[0])

    @pl.when(decoder)
    def _():
        arrived(ob.at[1], b_rs.at[1])

    for i in range(3):
        arrived(ob.at[4 + i], b_rs.at[4 + i])
        left = ob[0] if i == 0 else ob[key_slot]
        out_ref[i] = dot(left.reshape(512, 512), ob[4 + i].reshape(512, 512), TN)

    @pl.when(starts)
    def _():
        for m in range(MICRO):
            for k in range(4):
                sent_any(start_ref.at[m], i_ss.at[m, k], start_to[k])

    for mat in range(4):
        for k in range(4):
            sent_any(weights_ref.at[mat], g_ss.at[mat, k], gather_to[k])
    owners_sent(lambda b: xs.at[sel, :, b], 0)

    @pl.when(decoder)
    def _():
        owners_sent(lambda b: xs.at[0, :, b], 1)

    owners_sent(lambda b: xs.at[2, :, b], 2)
    owners_sent(lambda b: cs, 3)
    for i in range(3):
        owners_sent(lambda b: dd.at[:, i], 4 + i)

    def finish(m, carry):
        arrived(part.at[m, 0], q_ss.at[m])
        arrived(cs.at[m, 0], c_ss.at[m])
        arrived(dpart.at[m, 0], d_ss.at[m])
        arrived(dd.at[m, :, 0], dd_ss.at[m])
        arrived(cc.at[m, :, 0], cc_ss.at[m])

        @pl.when(decoder & (s < 7))
        def _():
            arrived(xs.at[0, m], f_ss.at[m])

        @pl.when(s < 7)
        def _():
            for k in range(3):
                arrived(ost.at[m, k], o_ss.at[m, k])
            for k in range(4):
                arrived(xn.at[m], n_ss.at[m, k])

        @pl.when((s > 0) & (s != 4))
        def _():
            for k in range(3):
                arrived(ust.at[m, k], u_ss.at[m, k])

        @pl.when(s > 0)
        def _():
            for k in range(4):
                arrived(gn.at[m], gn_ss.at[m, k])

        @pl.when(s >= 4)
        def _():
            for k in range(3):
                arrived(wst.at[m, k], w_ss.at[m, k])

        @pl.when(s > 4)
        def _():
            arrived(geout.at[m], e_ss.at[m])

        return carry

    lax.fori_loop(0, MICRO, finish, 0)


def per_device(enc_input, dec_input, cotangent, target_lengths, weights):
    section = lax.axis_index("section")
    micro_count, sequences, seq_length, feature_part = enc_input.shape
    scale = lax.rsqrt(jnp.float32(micro_count * lax.axis_size("dp") * sequences * seq_length))
    offsets = lax.broadcasted_iota(jnp.int32, (micro_count, sequences, seq_length), 2)
    live = (offsets < target_lengths[:, :, None]).astype(F32)
    seed = (cotangent.astype(F32) * live[..., None] * scale).astype(BF)
    start = jnp.where(section == 0, enc_input, jnp.where(section == 4, dec_input, seed))
    start = start.reshape(MICRO, 16, 2, 512).transpose(0, 2, 1, 3)
    dma = pltpu.SemaphoreType.DMA
    tile = (2, 16, 512)
    scratch = [
        pltpu.VMEM((4, 4, 512, 512), BF),
        pltpu.VMEM((3, MICRO, 4) + tile, BF),
        pltpu.VMEM((MICRO, 2, 16, 1792), F32),
        pltpu.VMEM((MICRO, 16, 1792), F32),
        pltpu.VMEM((MICRO, 16, 512), BF),
        pltpu.VMEM((MICRO, 16, 512), BF),
        pltpu.VMEM((MICRO, 16, 512), BF),
        pltpu.VMEM((MICRO, 2, 16, 16), F32),
        pltpu.VMEM((MICRO, 2, 16, 128), F32),
        pltpu.VMEM((MICRO,) + tile, BF),
        pltpu.VMEM((MICRO, 32, 512), F32),
        pltpu.VMEM((MICRO, 3, 32, 512), BF),
        pltpu.VMEM((MICRO, 3, 32, 512), BF),
        pltpu.VMEM((MICRO,) + tile, BF),
        pltpu.VMEM((MICRO,) + tile, F32),
        pltpu.VMEM((MICRO, 16, 512), F32),
        pltpu.VMEM((MICRO, 3) + tile, BF),
        pltpu.VMEM((MICRO, 2, 2, 16, 128), F32),
        pltpu.VMEM((MICRO, 32, 512), F32),
        pltpu.VMEM((MICRO, 3, 32, 512), BF),
        pltpu.VMEM((MICRO, 3, 32, 512), BF),
        pltpu.VMEM((MICRO, 32, 512), F32),
        pltpu.VMEM((MICRO, 3, 32, 512), BF),
        pltpu.VMEM((MICRO, 3, 32, 512), BF),
        pltpu.VMEM((MICRO,) + tile, BF),
        pltpu.VMEM((MICRO,) + tile, BF),
        pltpu.VMEM((MICRO,) + tile, BF),
        pltpu.VMEM((7, MICRO, 4) + tile, BF),
        dma((4, 4)), dma((4,)),
        dma((MICRO, 4)), dma((3, MICRO)),
        dma((MICRO,)),
        dma((MICRO,)), dma((MICRO,)),
        dma((MICRO,)), dma((MICRO,)),
        dma((MICRO, 3)), dma((MICRO,)),
        dma((MICRO, 4)),
        dma((MICRO,)), dma((MICRO,)),
        dma((MICRO,)), dma((MICRO,)),
        dma((MICRO,)), dma((MICRO,)),
        dma((MICRO, 3)), dma((MICRO,)),
        dma((MICRO, 3)), dma((MICRO,)),
        dma((MICRO,)), dma((MICRO,)),
        dma((MICRO, 4)),
        dma((7, 4)), dma((7,)),
    ]
    grads = pl.pallas_call(
        functools.partial(layer_kernel, 4096),
        out_shape=jax.ShapeDtypeStruct((4, 512, 512), F32),
        in_specs=[pl.BlockSpec(memory_space=pltpu.VMEM), pl.BlockSpec(memory_space=pl.ANY)],
        out_specs=pl.BlockSpec(memory_space=pltpu.VMEM),
        scratch_shapes=scratch,
        compiler_params=pltpu.CompilerParams(
            collective_id=0, has_side_effects=True, vmem_limit_bytes=48 << 20
        ),
        name="layers",
    )(start, weights[0])
    return grads[None]


def solution(mesh):
    in_specs = (
        P(None, "dp", None, "mp"),
        P(None, "dp", None, "mp"),
        P(None, "dp", None, "mp"),
        P(None, "dp"),
        P("section", None, "dp", "mp"),
    )
    return jax.shard_map(
        per_device,
        mesh=mesh,
        in_specs=in_specs,
        out_specs=P("section", None, "dp", "mp"),
        check_vma=False,
    )
```

time: 2440 us -> 443 us (0.18)
  waiting for transfers between devices: 1610 us -> 0 us
  Pallas kernels: 0 us -> 434 us
  blocking collectives: 422 us -> 0 us
  matrix products: 146 us -> 0 us
  starting transfers between devices: 98.5 us -> 0 us
  other arithmetic: 63.1 us -> 1.82 us
  local copies, waits for them, and re-layouts: 63.7 us -> 6.32 us
    reduce_scatter x23 -> x0, waiting for transfers between devices: 1220 us -> none  [the longest x22 892 us: head_sum(): lax.psum_scatter(head_terms.astype(jnp.bfloat16), 'mp', scatter_dimension...]
    pallas_call x0 -> x1, Pallas kernels: none -> 434 us  [per_device(): pl.pallas_call(functools.partial(layer_kernel, 4096), out_shape=jax.Shape...]
    all_gather x55 -> x0, blocking collectives: 422 us -> none  [the longest x22 174 us: collect(): lax.all_gather(key_side, 'mp', axis=1, tiled=True)]
    all_gather x1 -> x0, waiting for transfers between devices: 332 us -> none  [per_device(): full_weights = lax.all_gather(weights, 'dp', axis=2, tiled=True)]
    dot_general x76 -> x0, matrix products: 146 us -> none  [the longest x28 80.9 us: project(): jnp.dot(left_side, matrix, preferred_element_type=jnp.float32)]
    ppermute x44 -> x0, starting transfers between devices: 98.4 us -> none  [passed_along(): return lax.ppermute(value, axis, pairs)]
    ppermute x44 -> x0, waiting for transfers between devices: 51.4 us -> none  [passed_along(): return lax.ppermute(value, axis, pairs)]
    dynamic_update_slice x66 -> x0, other arithmetic: 28.7 us -> none  [store(): lax.dynamic_update_index_in_dim(stash_bank, jnp.where(active, update, cur...]
  transfers between devices with their start and end apart: 68 -> 0, of which waited for: 57 -> 0; matrix products, arithmetic and copies ran while one was open for 1% -> 0% of each run, Pallas kernels for 0% -> 0%
where the time goes in v1:
time: 443 us
  Pallas kernels  434 us (98%)
  local copies, waits for them, and re-layouts  6.32 us (1%)
    pallas_call x1, Pallas kernels, per_device(): pl.pallas_call(functools.partial(layer_kernel, 4096), out_shape=jax.Shape...  434 us

profile of v1, /device:TPU:1, one launch (start us, length us, event | category | flops | bytes accessed | tf_op | source)
XLA Modules:
  0.0 442.7 jit_solution(1664392287077634918)
XLA Ops:
  0.0 0.7 fusion.2
  0.7 1.1 fusion.1
  1.8 0.1 reshape.31
  1.9 0.0 copy-start
  1.9 1.6 copy-done
  3.5 434.5 %layers.1 = f32[4,512,512]{2,1,0:T(8,128)} custom-call(bf16[4,2,16,512]{3,2,1,0:T(8,128)(2,1)S(1)} %bitcast.9, bf16[4,512,512]{2,1,0:T(8,128)(2,1)S(1)} %bitcast.8), custom_call_target="tpu_custom_call" | custom-call | tf_op jit(solution)/shard_map/layers/pallas_call | solution.py:511
  438.0 4.6 %copy.10 = f32[1,4,512,512]{3,2,1,0:T(8,128)} copy(f32[1,4,512,512]{3,2,1,0:T(8,128)} %bitcast.10) | data formatting | bytes 8388608
  (1 shorter events, 0.0 us)
Async XLA Ops:
  1.9 1.6 copy-start

commit v2 on v1

--- a/solution.py
+++ b/solution.py
@@ -13,6 +13,7 @@
 BF = jnp.bfloat16
 F32 = jnp.float32
 MESH = pl.DeviceIdType.MESH
+ORDER = (2, 1, 3, 0)
 NT = (((1,), (1,)), ((), ()))
 NN = (((1,), (0,)), ((), ()))
 TN = (((0,), (0,)), ((), ()))
@@ -27,7 +28,8 @@
     start_ref, weights_ref, out_ref,
     w, xs, part, qrecv, qs, ks, vs, ps, rr, cs, oown, ost, orecv, xn,
     dpart, drecv, dd, cc, uown, ust, urecv, wown, wst, wrecv, gn, gein, geout, ob,
-    g_ss, g_rs, i_ss, x_rs, f_ss, q_ss, q_rs, c_ss, c_rs, o_ss, o_rs, n_ss,
+    ga_ss, ga_rs, gb_ss, gb_rs, gc_ss, gc_rs, i_ss, x_rs, f_ss, fp_ss, q_ss, q_rs, kv_ss, kv_rs,
+    c_ss, c_rs, o_ss, o_rs, n_ss,
     d_ss, d_rs, dd_ss, dd_rs, cc_ss, cc_rs, u_ss, u_rs, w_ss, w_rs, e_ss, e_rs, gn_ss,
     b_ss, b_rs,
 ):
@@ -37,10 +39,12 @@
     t = d // 2
     c = lax.rem(p, 2)
     j = 2 * (p // 2) + lax.rem(d, 2)
+    odd = lax.rem(t, 2)
     decoder = s >= 4
     sel = jnp.where(decoder, 1, 0)
     starts = (s == 0) | (s == 4) | (s == 7)
     start_stream = jnp.where(s == 0, 0, jnp.where(s == 4, 1, 2))
+    other = (d, p + 1 - 2 * c)
 
     def place(tt, jj, ccc):
         return 2 * tt + lax.rem(jj, 2), 2 * (jj // 2) + ccc
@@ -48,7 +52,14 @@
     def member(k):
         return place(t, lax.rem(j + k, 4), c)
 
-    gather_to = [place(k, p, d // 4) for k in range(4)]
+    def column(tt):
+        return 2 * tt + lax.rem(d, 2), p
+
+    collector = place(t, p, d // 4)
+    inner = t // 2 == c
+    beside = column(t + 1 - 2 * odd)
+    across = column(lax.rem(t + 3 - 2 * odd, 4))
+    senders = [place(k, p, d // 4) for k in range(4)]
     owner = [(4 * c + b, j) for b in range(4)]
     start_to = [place(t, jnp.int32(k), p // 2) for k in range(4)]
     start_from = [(2 * t + a, 2 * c + e) for a in range(2) for e in range(2)]
@@ -91,7 +102,14 @@
             ids["section"] = sec
         pl.semaphore_signal(bar, inc=1, device_id=ids, device_id_type=MESH)
 
-    greet((d, p + 1 - 2 * c))
+    def greet_other(dev):
+        @pl.when(jnp.logical_not(same(dev)))
+        def _():
+            greet(dev)
+
+    greet(other)
+    greet(beside)
+    greet(across)
     for k in range(1, 4):
         greet(member(k))
 
@@ -105,88 +123,153 @@
         for k in range(4):
             greet(member(k), s + 1)
 
-    for dev in gather_to + owner:
-        @pl.when(jnp.logical_not(same(dev)))
-        def _(dev=dev):
-            greet(dev)
+    for dev in senders:
+        greet_other(dev)
+
+    @pl.when(inner)
+    def _():
+        for e in range(2):
+            greet_other((2 * t + e, j))
 
     @pl.when(starts)
     def _():
         for dev in start_from:
-            @pl.when(jnp.logical_not(same(dev)))
-            def _(dev=dev):
-                greet(dev)
-
-    own_shard = sum(jnp.where(same(dev), 1, 0) for dev in gather_to)
-    own_start = sum(jnp.where(same(dev), 1, 0) for dev in start_to)
-    count = 4 + jnp.where(s > 0, 4, 0) + jnp.where(s < 7, 4, 0) + 8 - 2 * own_shard
-    count = count + jnp.where(starts, 4 - own_start, 0)
+            greet_other(dev)
+
+    def others(devs):
+        return sum(jnp.where(same(dev), 0, 1) for dev in devs)
+
+    count = 6 + jnp.where(s > 0, 4, 0) + jnp.where(s < 7, 4, 0) + others(owner)
+    count = count + others([collector]) + jnp.where(starts, others(start_to), 0)
     pl.semaphore_wait(bar, count)
+
+    for mat in range(4):
+        send_any(
+            weights_ref.at[mat], w.at[mat, lax.rem(d, 4)], ga_ss.at[mat], ga_rs.at[mat], collector
+        )
 
     @pl.when(starts)
     def _():
         for m in range(MICRO):
             for k in range(4):
-                send_any(
-                    start_ref.at[m],
-                    xs.at[start_stream, m, pl.ds(2 * lax.rem(p, 2), 2), lax.rem(d, 2)],
-                    i_ss.at[m, k], x_rs.at[start_stream, m], start_to[k],
-                )
-
-    for mat in range(4):
-        for k in range(4):
-            send_any(
-                weights_ref.at[mat], w.at[mat, lax.rem(d, 4)], g_ss.at[mat, k], g_rs.at[mat],
-                gather_to[k],
-            )
-    for mat in range(4):
-        arrived(w.at[mat], g_rs.at[mat])
+                for e in range(2):
+                    block = 2 * lax.rem(p, 2) + e
+                    send_any(
+                        start_ref.at[m, e], xs.at[start_stream, m, block, lax.rem(d, 2)],
+                        i_ss.at[m, k], x_rs.at[start_stream, m, block], start_to[k],
+                    )
+
+    def pair(mat, first):
+        return w.at[mat, pl.ds(2 * first, 2)]
+
+    @pl.when(inner)
+    def _():
+        def pass_on(mat):
+            arrived(pair(mat, 1 - odd), gb_rs.at[mat])
+            piece = w.at[mat, 2 * (1 - odd)]
+            remote(piece, piece, gc_ss.at[mat], gc_rs.at[mat], across).start()
+
+        for mat in range(4):
+            mine = pair(mat, odd)
+            arrived(mine, ga_rs.at[mat])
+            remote(mine, mine, gb_ss.at[mat, 0], gb_rs.at[mat], beside).start()
+            remote(mine, mine, gb_ss.at[mat, 1], gb_rs.at[mat], across).start()
+            if mat > 0:
+                pass_on(mat - 1)
+        pass_on(3)
+
+    @pl.when(jnp.logical_not(inner))
+    def _():
+        for mat in range(4):
+            arrived(pair(mat, 1 - odd), gb_rs.at[mat])
+            piece = w.at[mat, 2 * (1 - odd) + 1]
+            remote(piece, piece, gc_ss.at[mat], gc_rs.at[mat], beside).start()
+        for mat in range(4):
+            arrived(pair(mat, odd), gc_rs.at[mat])
 
     def rows(value):
         return value.reshape(32, 512)
 
+    def block_at(k):
+        return lax.rem(j + 4 - k, 4)
+
+    def project(m, stream, mats, start, ss, rs, relayed=None):
+        sums = [None] * len(mats)
+        squares = None
+        for k in ORDER:
+            block = block_at(k)
+            if k == 0 and relayed is not None:
+                @pl.when(jnp.logical_not(relayed))
+                def _():
+                    arrived(xs.at[stream, m, block], x_rs.at[stream, m, block])
+            else:
+                arrived(xs.at[stream, m, block], x_rs.at[stream, m, block])
+            left = rows(xs[stream, m, block])
+            wide = left.astype(F32)
+            square = jnp.sum(wide * wide, axis=-1, keepdims=True)
+            squares = square if squares is None else squares + square
+            for i, mat in enumerate(mats):
+                term = dot(left, w[mat, block])
+                sums[i] = term if sums[i] is None else sums[i] + term
+        squares = jnp.broadcast_to(squares, (32, 128)).reshape(2, 16, 128)
+        for i, mat in enumerate(mats):
+            first = (0, 640, 1152)[mat]
+            part[m, :, :, first:first + 512] = sums[i].reshape(2, 16, 512)
+        if 0 in mats:
+            part[m, :, :, 512:640] = squares
+        if 1 in mats:
+            part[m, :, :, 1664:1792] = squares
+        cols = pl.ds(*start)
+        remote(part.at[m, 1 - c, :, cols], qrecv.at[m, :, cols], ss.at[m], rs.at[m], other).start()
+
+    def project_all(m):
+        project(m, 0, (0, 1, 2), (0, 1792), q_ss, q_rs)
+
+    def project_query(m):
+        project(m, 1, (0,), (0, 640), q_ss, q_rs)
+
+    def project_key(m):
+        project(m, 0, (1, 2), (640, 1152), kv_ss, kv_rs, s > 4)
+
+        @pl.when(s == 4)
+        def _():
+            onward(m)
+
+    def onward(m):
+        remote(
+            xs.at[0, m, j], xs.at[0, m, j], f_ss.at[m], x_rs.at[0, m, j], (d, p), s + 1
+        ).start()
+
+    def relay(m):
+        arrived(xs.at[0, m, j], x_rs.at[0, m, j])
+
+        @pl.when(s < 7)
+        def _():
+            onward(m)
+
+        for k in (2, 1, 3):
+            remote(
+                xs.at[0, m, j], xs.at[0, m, j], fp_ss.at[m, k - 1], x_rs.at[0, m, j], member(k)
+            ).start()
+
     def attend(m):
-        arrived(xs.at[0, m], x_rs.at[0, m])
-
         @pl.when(decoder)
         def _():
-            @pl.when(s < 7)
-            def _():
-                remote(
-                    xs.at[0, m], xs.at[0, m], f_ss.at[m], x_rs.at[0, m], (d, p), s + 1
-                ).start()
-
-            arrived(xs.at[1, m], x_rs.at[1, m])
-
-        sums = [None, None, None]
-        squares = [None, None]
-        for b in range(4):
-            query = rows(xs[sel, m, b])
-            key = rows(xs[0, m, b])
-            for i, left in enumerate((query, key, key)):
-                term = dot(left, w[i, b])
-                sums[i] = term if b == 0 else sums[i] + term
-            for i, left in enumerate((query, key)):
-                wide = left.astype(F32)
-                term = jnp.sum(wide * wide, axis=-1, keepdims=True)
-                squares[i] = term if b == 0 else squares[i] + term
-        for i in range(3):
-            part[m, :, :, i * 512:(i + 1) * 512] = sums[i].reshape(2, 16, 512)
-        for i in range(2):
-            part[m, :, :, 1536 + i * 128:1664 + i * 128] = jnp.broadcast_to(
-                squares[i], (32, 128)
-            ).reshape(2, 16, 128)
-        other = (d, p + 1 - 2 * c)
-        remote(part.at[m, 1 - c], qrecv.at[m], q_ss.at[m], q_rs.at[m], other).start()
-        arrived(qrecv.at[m], q_rs.at[m])
+            arrived(qrecv.at[m, :, pl.ds(0, 640)], q_rs.at[m])
+            arrived(qrecv.at[m, :, pl.ds(640, 1152)], kv_rs.at[m])
+
+        @pl.when(jnp.logical_not(decoder))
+        def _():
+            arrived(qrecv.at[m], q_rs.at[m])
+
         total = part[m, c] + qrecv[m]
-        factor_q = lax.rsqrt(total[:, 1536:1537] * (1.0 / width) + EPSILON)
+        factor_q = lax.rsqrt(total[:, 512:513] * (1.0 / width) + EPSILON)
         factor_k = lax.rsqrt(total[:, 1664:1665] * (1.0 / width) + EPSILON)
         rr[m, 0] = jnp.broadcast_to(factor_q, (16, 128))
         rr[m, 1] = jnp.broadcast_to(factor_k, (16, 128))
         query = (total[:, :512] * factor_q).astype(BF)
-        key = (total[:, 512:1024] * factor_k).astype(BF)
-        value = (total[:, 1024:1536] * factor_k).astype(BF)
+        key = (total[:, 640:1152] * factor_k).astype(BF)
+        value = (total[:, 1152:1664] * factor_k).astype(BF)
         qs[m] = query
         ks[m] = key
         vs[m] = value
@@ -204,7 +287,7 @@
         @pl.when(s < 7)
         def _():
             context = rows(cs[m])
-            for k in (1, 2, 3, 0):
+            for k in ORDER:
                 term = dot(context, w[3, lax.rem(j + k, 4)], NT)
                 if k == 0:
                     oown[m] = term
@@ -216,78 +299,89 @@
                     ).start()
 
     def advance(m):
+        total = rows(xs[sel, m, j]).astype(F32) + oown[m]
         arrived(orecv.at[m], o_rs.at[m])
-        total = rows(xs[sel, m, j]).astype(F32) + oown[m]
         for k in range(3):
             total = total + orecv[m, k].astype(F32)
         xn[m] = total.astype(BF).reshape(2, 16, 512)
-        for k in range(4):
+        for k in ORDER:
             remote(
-                xn.at[m], xs.at[sel, m, j], n_ss.at[m, k], x_rs.at[sel, m], member(k), s + 1
+                xn.at[m], xs.at[sel, m, j], n_ss.at[m, k], x_rs.at[sel, m, j], member(k), s + 1
             ).start()
 
-    def forward_step(i, carry):
+    def forward_step(i):
+        @pl.when((i < MICRO) & (s < 4))
+        def _():
+            project_all(i)
+
+        @pl.when((i < MICRO - 1) & (s == 4))
+        def _():
+            project_query(i + 1)
+
+        @pl.when(((i < MICRO) & (s == 4)) | ((i < MICRO - 1) & (s > 4)))
+        def _():
+            project_key(i + jnp.where(s > 4, 1, 0))
+
+        @pl.when((i < MICRO) & (s > 4))
+        def _():
+            project_query(i)
+
+            @pl.when(i < MICRO - 2)
+            def _():
+                relay(i + 2)
+
+        @pl.when((i > 0) & (s < 7))
+        def _():
+            advance(i - 1)
+
         @pl.when(i < MICRO)
         def _():
             attend(i)
 
-        @pl.when((i > 0) & (s < 7))
-        def _():
-            advance(i - 1)
-
-        return carry
-
-    lax.fori_loop(0, MICRO + 1, forward_step, 0)
-
-    def to_owners(src_of, slot):
+    def to_owners(src_of, slot, m=None):
         for b in range(4):
-            send_any(src_of(b), ob.at[slot, :, t], b_ss.at[slot, b], b_rs.at[slot], owner[b])
+            dst = ob.at[slot, :, t] if m is None else ob.at[slot, m, t]
+            send_any(src_of(b), dst, b_ss.at[slot, b], b_rs.at[slot], owner[b])
 
     def owners_sent(src_of, slot):
         for b in range(4):
             sent_any(src_of(b), b_ss.at[slot, b], owner[b])
 
-    to_owners(lambda b: xs.at[sel, :, b], 0)
-
-    @pl.when(decoder)
-    def _():
-        to_owners(lambda b: xs.at[0, :, b], 1)
-
-    to_owners(lambda b: cs, 3)
+    def project_back(m):
+        total = None
+        for k in ORDER:
+            block = block_at(k)
+            arrived(xs.at[2, m, block], x_rs.at[2, m, block])
+            term = dot(rows(xs[2, m, block]), w[3, block])
+            total = term if total is None else total + term
+        dpart[m] = total.reshape(2, 16, 512)
+        remote(dpart.at[m, 1 - c], drecv.at[m], d_ss.at[m], d_rs.at[m], other).start()
 
     def attend_back(m):
-        arrived(xs.at[2, m], x_rs.at[2, m])
-        total = None
-        for b in range(4):
-            term = dot(rows(xs[2, m, b]), w[3, b])
-            total = term if b == 0 else total + term
-        dpart[m] = total.reshape(2, 16, 512)
-        other = (d, p + 1 - 2 * c)
-        remote(dpart.at[m, 1 - c], drecv.at[m], d_ss.at[m], d_rs.at[m], other).start()
+        query, key, value = qs[m], ks[m], vs[m]
         arrived(drecv.at[m], d_rs.at[m])
         grad = (dpart[m, c] + drecv[m]).astype(BF)
-        query, key, value = qs[m], ks[m], vs[m]
         pieces = [[], [], []]
         for h in range(2):
             cols = slice(h * HEAD_DIM, (h + 1) * HEAD_DIM)
             weight = ps[m, h]
             grad_weight = dot(grad[:, cols], value[:, cols], NT)
             pieces[2].append(dot(weight.astype(BF), grad[:, cols], TN))
-            inner = jnp.sum(grad_weight * weight, axis=-1, keepdims=True)
-            scores = (weight * (grad_weight - inner) * HEAD_DIM ** (-0.5)).astype(BF)
+            inside = jnp.sum(grad_weight * weight, axis=-1, keepdims=True)
+            scores = (weight * (grad_weight - inside) * HEAD_DIM ** (-0.5)).astype(BF)
             pieces[0].append(dot(scores, key[:, cols]))
             pieces[1].append(dot(scores, query[:, cols], TN))
         grads = [jnp.concatenate(piece, axis=1) for piece in pieces]
         factors = [rr[m, 0][:, :1], rr[m, 1][:, :1], rr[m, 1][:, :1]]
+        for i in range(3):
+            dd[m, i, c] = (grads[i] * factors[i]).astype(BF)
+        remote(dd.at[m, :, c], dd.at[m, :, c], dd_ss.at[m], dd_rs.at[m], other).start()
         means = [
             jnp.sum(g * v.astype(F32), axis=-1, keepdims=True) * (1.0 / width)
             for g, v in zip(grads, (query, key, value))
         ]
-        for i in range(3):
-            dd[m, i, c] = (grads[i] * factors[i]).astype(BF)
         cc[m, 0, c] = jnp.broadcast_to(means[0] * factors[0] * factors[0], (16, 128))
         cc[m, 1, c] = jnp.broadcast_to((means[1] + means[2]) * factors[1] * factors[1], (16, 128))
-        remote(dd.at[m, :, c], dd.at[m, :, c], dd_ss.at[m], dd_rs.at[m], other).start()
         remote(cc.at[m, :, c], cc.at[m, :, c], cc_ss.at[m], cc_rs.at[m], other).start()
         arrived(dd.at[m, :, c], dd_rs.at[m])
         arrived(cc.at[m, :, c], cc_rs.at[m])
@@ -295,7 +389,7 @@
         def spread(pairs, stream, kinds, own, stage, recv, ss, rs):
             lefts = [rows(dd[m, i]) for i in pairs]
             shift = sum(cc[m, i].reshape(32, 128)[:, :1] for i in kinds)
-            for k in (1, 2, 3, 0):
+            for k in ORDER:
                 block = lax.rem(j + k, 4)
                 term = -rows(xs[stream, m, block]).astype(F32) * shift
                 for i, left in zip(pairs, lefts):
@@ -321,59 +415,107 @@
             spread((1, 2), 0, (1,), wown, wst, wrecv, w_ss, w_rs)
 
     def hand_back(m):
-        for k in range(4):
+        for k in ORDER:
             remote(
-                gn.at[m], xs.at[2, m, j], gn_ss.at[m, k], x_rs.at[2, m], member(k), s - 1
+                gn.at[m], xs.at[2, m, j], gn_ss.at[m, k], x_rs.at[2, m, j], member(k), s - 1
             ).start()
 
     def advance_back(m):
-        @pl.when(s != 4)
-        def _():
-            arrived(urecv.at[m], u_rs.at[m])
-            total = rows(xs[2, m, j]).astype(F32) + uown[m]
-            for k in range(3):
-                total = total + urecv[m, k].astype(F32)
-            gn[m] = total.astype(BF).reshape(2, 16, 512)
+        total = rows(xs[2, m, j]).astype(F32) + uown[m]
+        arrived(urecv.at[m], u_rs.at[m])
+        for k in range(3):
+            total = total + urecv[m, k].astype(F32)
+        gn[m] = total.astype(BF).reshape(2, 16, 512)
+        hand_back(m)
+
+    def advance_key(m):
+        arrived(wrecv.at[m], w_rs.at[m])
+        total = wown[m]
+        for k in range(3):
+            total = total + wrecv[m, k].astype(F32)
+        geout[m] = total.astype(BF).reshape(2, 16, 512)
+
+        @pl.when(s < 7)
+        def _():
+            arrived(gein.at[m], e_rs.at[m])
+            geout[m] = (total + rows(gein[m]).astype(F32)).astype(BF).reshape(2, 16, 512)
+
+        @pl.when(s > 4)
+        def _():
+            remote(geout.at[m], gein.at[m], e_ss.at[m], e_rs.at[m], (d, p), s - 1).start()
+
+        @pl.when(s == 4)
+        def _():
+            gn[m] = geout[m]
             hand_back(m)
 
-        @pl.when(s >= 4)
-        def _():
-            arrived(wrecv.at[m], w_rs.at[m])
-            total = wown[m]
-            for k in range(3):
-                total = total + wrecv[m, k].astype(F32)
-            geout[m] = total.astype(BF).reshape(2, 16, 512)
-
-            @pl.when(s < 7)
+    def backward_step(i):
+        @pl.when(i < MICRO)
+        def _():
+            project_back(i)
+
+        @pl.when((i > 0) & (s > 0) & (s != 4))
+        def _():
+            advance_back(i - 1)
+
+        @pl.when((i > 0) & (s == 4))
+        def _():
+            advance_key(i - 1)
+
+        @pl.when(i < MICRO)
+        def _():
+            attend_back(i)
+
+            @pl.when(s == 0)
             def _():
-                arrived(gein.at[m], e_rs.at[m])
-                geout[m] = (total + rows(gein[m]).astype(F32)).astype(BF).reshape(2, 16, 512)
-
-            @pl.when(s > 4)
+                to_owners(lambda b: xs.at[2, i, b], 2, i)
+                for k in range(3):
+                    to_owners(lambda b: dd.at[i, k], 4 + k, i)
+
+        @pl.when((i > 0) & (s > 4))
+        def _():
+            advance_key(i - 1)
+
+    @pl.when(s == 4)
+    def _():
+        project_query(0)
+
+    @pl.when(s > 4)
+    def _():
+        relay(0)
+        relay(1)
+        project_key(0)
+
+    def step(n, carry):
+        @pl.when(n <= MICRO)
+        def _():
+            forward_step(n)
+
+        @pl.when(n == MICRO + 1)
+        def _():
+            to_owners(lambda b: xs.at[sel, :, b], 0)
+
+            @pl.when(decoder)
             def _():
-                remote(geout.at[m], gein.at[m], e_ss.at[m], e_rs.at[m], (d, p), s - 1).start()
-
-            @pl.when(s == 4)
-            def _():
-                gn[m] = geout[m]
-                hand_back(m)
-
-    def backward_step(i, carry):
-        @pl.when(i < MICRO)
-        def _():
-            attend_back(i)
-
-        @pl.when((i > 0) & (s > 0))
-        def _():
-            advance_back(i - 1)
+                to_owners(lambda b: xs.at[0, :, b], 1)
+
+            to_owners(lambda b: cs, 3)
+
+        back = n - jnp.where(s == 7, 0, MICRO + 1)
+
+        @pl.when((back >= 0) & (back <= MICRO))
+        def _():
+            backward_step(back)
 
         return carry
 
-    lax.fori_loop(0, MICRO + 1, backward_step, 0)
-
-    to_owners(lambda b: xs.at[2, :, b], 2)
-    for i in range(3):
-        to_owners(lambda b: dd.at[:, i], 4 + i)
+    lax.fori_loop(0, 2 * MICRO + 2, step, 0)
+
+    @pl.when(s > 0)
+    def _():
+        to_owners(lambda b: xs.at[2, :, b], 2)
+        for i in range(3):
+            to_owners(lambda b: dd.at[:, i], 4 + i)
 
     key_slot = jnp.where(decoder, 1, 0)
     arrived(ob.at[3], b_rs.at[3])
@@ -397,8 +539,14 @@
                 sent_any(start_ref.at[m], i_ss.at[m, k], start_to[k])
 
     for mat in range(4):
-        for k in range(4):
-            sent_any(weights_ref.at[mat], g_ss.at[mat, k], gather_to[k])
+        sent_any(weights_ref.at[mat], ga_ss.at[mat], collector)
+        arrived(w.at[mat, 0], gc_ss.at[mat])
+
+        @pl.when(inner)
+        def _():
+            for k in range(2):
+                arrived(pair(mat, 0), gb_ss.at[mat, k])
+
     owners_sent(lambda b: xs.at[sel, :, b], 0)
 
     @pl.when(decoder)
@@ -411,7 +559,15 @@
         owners_sent(lambda b: dd.at[:, i], 4 + i)
 
     def finish(m, carry):
-        arrived(part.at[m, 0], q_ss.at[m])
+        @pl.when(decoder)
+        def _():
+            arrived(part.at[m, 0, :, pl.ds(0, 640)], q_ss.at[m])
+            arrived(part.at[m, 0, :, pl.ds(640, 1152)], kv_ss.at[m])
+
+        @pl.when(jnp.logical_not(decoder))
+        def _():
+            arrived(part.at[m, 0], q_ss.at[m])
+
         arrived(cs.at[m, 0], c_ss.at[m])
         arrived(dpart.at[m, 0], d_ss.at[m])
         arrived(dd.at[m, :, 0], dd_ss.at[m])
@@ -419,7 +575,12 @@
 
         @pl.when(decoder & (s < 7))
         def _():
-            arrived(xs.at[0, m], f_ss.at[m])
+            arrived(xs.at[0, m, 0], f_ss.at[m])
+
+        @pl.when(s > 4)
+        def _():
+            for k in range(3):
+                arrived(xs.at[0, m, 0], fp_ss.at[m, k])
 
         @pl.when(s < 7)
         def _():
@@ -492,9 +653,12 @@
         pltpu.VMEM((MICRO,) + tile, BF),
         pltpu.VMEM((MICRO,) + tile, BF),
         pltpu.VMEM((7, MICRO, 4) + tile, BF),
-        dma((4, 4)), dma((4,)),
-        dma((MICRO, 4)), dma((3, MICRO)),
-        dma((MICRO,)),
+        dma((4,)), dma((4,)),
+        dma((4, 2)), dma((4,)),
+        dma((4,)), dma((4,)),
+        dma((MICRO, 4)), dma((3, MICRO, 4)),
+        dma((MICRO,)), dma((MICRO, 3)),
+        dma((MICRO,)), dma((MICRO,)),
         dma((MICRO,)), dma((MICRO,)),
         dma((MICRO,)), dma((MICRO,)),
         dma((MICRO, 3)), dma((MICRO,)),

time: 443 us -> 348 us (0.79)
  the two profiles are of different devices: /device:TPU:1 before, /device:TPU:32 now
where the time goes in v2:
time: 348 us; the launch traced here: 347 us
  Pallas kernels  339 us (97%)
  local copies, waits for them, and re-layouts  6.32 us (2%)
    pallas_call x1, Pallas kernels, per_device(): pl.pallas_call(functools.partial(layer_kernel, 4096), out_shape=jax.Shape...  339 us

profile of v2, /device:TPU:32, one launch (start us, length us, event | category | flops | bytes accessed | tf_op | source)
XLA Modules:
  0.0 347.4 jit_solution(9956934952498844361)
XLA Ops:
  0.0 0.7 fusion.2
  0.7 1.0 fusion.1
  1.8 0.1 reshape.31
  1.9 0.0 copy-start
  1.9 1.6 copy-done
  3.5 339.3 %layers.1 = f32[4,512,512]{2,1,0:T(8,128)} custom-call(bf16[4,2,16,512]{3,2,1,0:T(8,128)(2,1)S(1)} %bitcast.9, bf16[4,512,512]{2,1,0:T(8,128)(2,1)S(1)} %bitcast.8), custom_call_target="tpu_custom_call" | custom-call | tf_op jit(solution)/shard_map/layers/pallas_call | solution.py:675
  342.7 4.6 %copy.10 = f32[1,4,512,512]{3,2,1,0:T(8,128)} copy(f32[1,4,512,512]{3,2,1,0:T(8,128)} %bitcast.10) | data formatting | bytes 8388608
  (1 shorter events, 0.0 us)
Async XLA Ops:
  1.9 1.6 copy-start

commit v3 on v2

--- a/solution.py
+++ b/solution.py
@@ -24,11 +24,11 @@
 
 
 def layer_kernel(
-    width,
-    start_ref, weights_ref, out_ref,
-    w, xs, part, qrecv, qs, ks, vs, ps, rr, cs, oown, ost, orecv, xn,
+    width, loss_scale,
+    lengths_ref, enc_ref, dec_ref, cot_ref, weights_ref, out_ref,
+    w, xs, seed, seed_in, part, qrecv, qs, ks, vs, ps, rr, cs, oown, ost, orecv, xn,
     dpart, drecv, dd, cc, uown, ust, urecv, wown, wst, wrecv, gn, gein, geout, ob,
-    ga_ss, ga_rs, gb_ss, gb_rs, gc_ss, gc_rs, i_ss, x_rs, f_ss, fp_ss, q_ss, q_rs, kv_ss, kv_rs,
+    s_sem, ga_ss, ga_rs, gb_ss, gb_rs, gc_ss, gc_rs, i_ss, x_rs, f_ss, fp_ss, q_ss, q_rs, kv_ss, kv_rs,
     c_ss, c_rs, o_ss, o_rs, n_ss,
     d_ss, d_rs, dd_ss, dd_rs, cc_ss, cc_rs, u_ss, u_rs, w_ss, w_rs, e_ss, e_rs, gn_ss,
     b_ss, b_rs,
@@ -43,7 +43,6 @@
     decoder = s >= 4
     sel = jnp.where(decoder, 1, 0)
     starts = (s == 0) | (s == 4) | (s == 7)
-    start_stream = jnp.where(s == 0, 0, jnp.where(s == 4, 1, 2))
     other = (d, p + 1 - 2 * c)
 
     def place(tt, jj, ccc):
@@ -143,49 +142,112 @@
     count = count + others([collector]) + jnp.where(starts, others(start_to), 0)
     pl.semaphore_wait(bar, count)
 
-    for mat in range(4):
+    def shards(piece, first, number):
+        return w.at[piece // 2, pl.ds(first, number), pl.ds(256 * lax.rem(piece, 2), 256)]
+
+    def shard(piece, which):
+        return w.at[piece // 2, which, pl.ds(256 * lax.rem(piece, 2), 256)]
+
+    def own_shard(piece):
+        return weights_ref.at[0, piece // 2, pl.ds(256 * lax.rem(piece, 2), 256)]
+
+    def give(piece, carry):
         send_any(
-            weights_ref.at[mat], w.at[mat, lax.rem(d, 4)], ga_ss.at[mat], ga_rs.at[mat], collector
+            own_shard(piece), shard(piece, lax.rem(d, 4)), ga_ss.at[piece], ga_rs.at[piece],
+            collector,
         )
-
-    @pl.when(starts)
-    def _():
+        return carry
+
+    lax.fori_loop(0, 8, give, 0)
+
+    def begin(src_of, stream):
         for m in range(MICRO):
             for k in range(4):
                 for e in range(2):
                     block = 2 * lax.rem(p, 2) + e
                     send_any(
-                        start_ref.at[m, e], xs.at[start_stream, m, block, lax.rem(d, 2)],
-                        i_ss.at[m, k], x_rs.at[start_stream, m, block], start_to[k],
+                        src_of(m, e), xs.at[stream, m, block, lax.rem(d, 2)],
+                        i_ss.at[m, k], x_rs.at[stream, m, block], start_to[k],
                     )
 
-    def pair(mat, first):
-        return w.at[mat, pl.ds(2 * first, 2)]
-
-    @pl.when(inner)
-    def _():
-        def pass_on(mat):
-            arrived(pair(mat, 1 - odd), gb_rs.at[mat])
-            piece = w.at[mat, 2 * (1 - odd)]
-            remote(piece, piece, gc_ss.at[mat], gc_rs.at[mat], across).start()
-
-        for mat in range(4):
-            mine = pair(mat, odd)
-            arrived(mine, ga_rs.at[mat])
-            remote(mine, mine, gb_ss.at[mat, 0], gb_rs.at[mat], beside).start()
-            remote(mine, mine, gb_ss.at[mat, 1], gb_rs.at[mat], across).start()
-            if mat > 0:
-                pass_on(mat - 1)
-        pass_on(3)
-
-    @pl.when(jnp.logical_not(inner))
-    def _():
-        for mat in range(4):
-            arrived(pair(mat, 1 - odd), gb_rs.at[mat])
-            piece = w.at[mat, 2 * (1 - odd) + 1]
-            remote(piece, piece, gc_ss.at[mat], gc_rs.at[mat], beside).start()
-        for mat in range(4):
-            arrived(pair(mat, odd), gc_rs.at[mat])
+    @pl.when(s == 0)
+    def _():
+        begin(lambda m, e: enc_ref.at[m, 0, :, pl.ds(512 * e, 512)], 0)
+
+    @pl.when(s == 4)
+    def _():
+        begin(lambda m, e: dec_ref.at[m, 0, :, pl.ds(512 * e, 512)], 1)
+
+    @pl.when(s == 7)
+    def _():
+        loss = pltpu.make_async_copy(cot_ref.at[:, 0], seed_in, s_sem)
+        loss.start()
+        loss.wait()
+        for m in range(MICRO):
+            offsets = lax.broadcasted_iota(jnp.int32, (16, 1024), 0)
+            live = jnp.where(offsets < lengths_ref[m, 0], loss_scale, 0.0)
+            value = (seed_in[m].astype(F32) * live).astype(BF)
+            for e in range(2):
+                seed[m, e] = value[:, 512 * e:512 * e + 512]
+        begin(lambda m, e: seed.at[m, e], 2)
+
+    def pass_on(piece):
+        arrived(shards(piece, 2 * (1 - odd), 2), gb_rs.at[piece])
+        half = shard(piece, 2 * (1 - odd))
+        remote(half, half, gc_ss.at[piece], gc_rs.at[piece], across).start()
+
+    def collected(piece):
+        mine = shards(piece, 2 * odd, 2)
+        arrived(mine, ga_rs.at[piece])
+        remote(mine, mine, gb_ss.at[piece, 0], gb_rs.at[piece], beside).start()
+        remote(mine, mine, gb_ss.at[piece, 1], gb_rs.at[piece], across).start()
+
+    def swap(piece):
+        arrived(shards(piece, 2 * (1 - odd), 2), gb_rs.at[piece])
+        half = shard(piece, 2 * (1 - odd) + 1)
+        remote(half, half, gc_ss.at[piece], gc_rs.at[piece], beside).start()
+
+    def swapped(piece):
+        arrived(shards(piece, 2 * odd, 2), gc_rs.at[piece])
+
+    def gather_most():
+        @pl.when(inner)
+        def _():
+            def one(piece, carry):
+                collected(piece)
+
+                @pl.when(piece > 0)
+                def _():
+                    pass_on(piece - 1)
+
+                return carry
+
+            lax.fori_loop(0, 7, one, 0)
+            collected(7)
+
+        @pl.when(jnp.logical_not(inner))
+        def _():
+            def one(piece, carry):
+                swap(piece)
+                return carry
+
+            def other_one(piece, carry):
+                swapped(piece)
+                return carry
+
+            lax.fori_loop(0, 6, one, 0)
+            lax.fori_loop(0, 6, other_one, 0)
+
+    def gather_one(piece):
+        @pl.when(inner)
+        def _():
+            pass_on(piece)
+
+        @pl.when(jnp.logical_not(inner))
+        def _():
+            swap(piece)
+
+    gather_most()
 
     def rows(value):
         return value.reshape(32, 512)
@@ -282,6 +344,8 @@
             contexts.append(dot(weight, value[:, cols]).astype(BF))
         cs[m, c] = jnp.concatenate(contexts, axis=1)
         remote(cs.at[m, c], cs.at[m, c], c_ss.at[m], c_rs.at[m], other).start()
+
+    def output(m):
         arrived(cs.at[m, c], c_rs.at[m])
 
         @pl.when(s < 7)
@@ -310,7 +374,7 @@
             ).start()
 
     def forward_step(i):
-        @pl.when((i < MICRO) & (s < 4))
+        @pl.when((i < MICRO) & (s < 4) & (s > 0))
         def _():
             project_all(i)
 
@@ -336,7 +400,11 @@
 
         @pl.when(i < MICRO)
         def _():
-            attend(i)
+            @pl.when(s > 0)
+            def _():
+                attend(i)
+
+            output(i)
 
     def to_owners(src_of, slot, m=None):
         for b in range(4):
@@ -466,7 +534,7 @@
         def _():
             attend_back(i)
 
-            @pl.when(s == 0)
+            @pl.when(s < 2)
             def _():
                 to_owners(lambda b: xs.at[2, i, b], 2, i)
                 for k in range(3):
@@ -476,6 +544,25 @@
         def _():
             advance_key(i - 1)
 
+    def early(what):
+        @pl.when(s == 0)
+        def _():
+            def one(m, carry):
+                what(m)
+                return carry
+
+            lax.fori_loop(0, MICRO, one, 0)
+
+    early(project_all)
+    gather_one(6)
+    early(attend)
+    gather_one(7)
+
+    @pl.when(jnp.logical_not(inner))
+    def _():
+        swapped(6)
+        swapped(7)
+
     @pl.when(s == 4)
     def _():
         project_query(0)
@@ -511,7 +598,7 @@
 
     lax.fori_loop(0, 2 * MICRO + 2, step, 0)
 
-    @pl.when(s > 0)
+    @pl.when(s > 1)
     def _():
         to_owners(lambda b: xs.at[2, :, b], 2)
         for i in range(3):
@@ -520,7 +607,7 @@
     key_slot = jnp.where(decoder, 1, 0)
     arrived(ob.at[3], b_rs.at[3])
     arrived(ob.at[2], b_rs.at[2])
-    out_ref[3] = dot(ob[2].reshape(512, 512), ob[3].reshape(512, 512), TN)
+    out_ref[3] = dot(ob[2].reshape(512, 512), ob[3].reshape(512, 512), TN).astype(BF)
     arrived(ob.at[0], b_rs.at[0])
 
     @pl.when(decoder)
@@ -530,22 +617,26 @@
     for i in range(3):
         arrived(ob.at[4 + i], b_rs.at[4 + i])
         left = ob[0] if i == 0 else ob[key_slot]
-        out_ref[i] = dot(left.reshape(512, 512), ob[4 + i].reshape(512, 512), TN)
+        out_ref[i] = dot(left.reshape(512, 512), ob[4 + i].reshape(512, 512), TN).astype(BF)
 
     @pl.when(starts)
     def _():
         for m in range(MICRO):
             for k in range(4):
-                sent_any(start_ref.at[m], i_ss.at[m, k], start_to[k])
-
-    for mat in range(4):
-        sent_any(weights_ref.at[mat], ga_ss.at[mat], collector)
-        arrived(w.at[mat, 0], gc_ss.at[mat])
+                sent_any(seed.at[m], i_ss.at[m, k], start_to[k])
+
+    def given(piece, carry):
+        sent_any(own_shard(piece), ga_ss.at[piece], collector)
+        arrived(shard(piece, 0), gc_ss.at[piece])
 
         @pl.when(inner)
         def _():
             for k in range(2):
-                arrived(pair(mat, 0), gb_ss.at[mat, k])
+                arrived(shards(piece, 0, 2), gb_ss.at[piece, k])
+
+        return carry
+
+    lax.fori_loop(0, 8, given, 0)
 
     owners_sent(lambda b: xs.at[sel, :, b], 0)
 
@@ -614,19 +705,14 @@
 
 
 def per_device(enc_input, dec_input, cotangent, target_lengths, weights):
-    section = lax.axis_index("section")
-    micro_count, sequences, seq_length, feature_part = enc_input.shape
-    scale = lax.rsqrt(jnp.float32(micro_count * lax.axis_size("dp") * sequences * seq_length))
-    offsets = lax.broadcasted_iota(jnp.int32, (micro_count, sequences, seq_length), 2)
-    live = (offsets < target_lengths[:, :, None]).astype(F32)
-    seed = (cotangent.astype(F32) * live[..., None] * scale).astype(BF)
-    start = jnp.where(section == 0, enc_input, jnp.where(section == 4, dec_input, seed))
-    start = start.reshape(MICRO, 16, 2, 512).transpose(0, 2, 1, 3)
+    tokens = MICRO * lax.axis_size("dp") * enc_input.shape[1] * enc_input.shape[2]
     dma = pltpu.SemaphoreType.DMA
     tile = (2, 16, 512)
     scratch = [
         pltpu.VMEM((4, 4, 512, 512), BF),
         pltpu.VMEM((3, MICRO, 4) + tile, BF),
+        pltpu.VMEM((MICRO, 2, 16, 512), BF),
+        pltpu.VMEM((MICRO, 16, 1024), BF),
         pltpu.VMEM((MICRO, 2, 16, 1792), F32),
         pltpu.VMEM((MICRO, 16, 1792), F32),
         pltpu.VMEM((MICRO, 16, 512), BF),
@@ -653,9 +739,10 @@
         pltpu.VMEM((MICRO,) + tile, BF),
         pltpu.VMEM((MICRO,) + tile, BF),
         pltpu.VMEM((7, MICRO, 4) + tile, BF),
-        dma((4,)), dma((4,)),
-        dma((4, 2)), dma((4,)),
-        dma((4,)), dma((4,)),
+        dma,
+        dma((8,)), dma((8,)),
+        dma((8, 2)), dma((8,)),
+        dma((8,)), dma((8,)),
         dma((MICRO, 4)), dma((3, MICRO, 4)),
         dma((MICRO,)), dma((MICRO, 3)),
         dma((MICRO,)), dma((MICRO,)),
@@ -673,17 +760,17 @@
         dma((7, 4)), dma((7,)),
     ]
     grads = pl.pallas_call(
-        functools.partial(layer_kernel, 4096),
-        out_shape=jax.ShapeDtypeStruct((4, 512, 512), F32),
-        in_specs=[pl.BlockSpec(memory_space=pltpu.VMEM), pl.BlockSpec(memory_space=pl.ANY)],
+        functools.partial(layer_kernel, 4096, float(tokens) ** (-0.5)),
+        out_shape=jax.ShapeDtypeStruct((4, 512, 512), BF),
+        in_specs=[pl.BlockSpec(memory_space=pltpu.SMEM)] + [pl.BlockSpec(memory_space=pl.ANY)] * 4,
         out_specs=pl.BlockSpec(memory_space=pltpu.VMEM),
         scratch_shapes=scratch,
         compiler_params=pltpu.CompilerParams(
-            collective_id=0, has_side_effects=True, vmem_limit_bytes=48 << 20
+            collective_id=0, has_side_effects=True, vmem_limit_bytes=60 << 20
         ),
         name="layers",
-    )(start, weights[0])
-    return grads[None]
+    )(target_lengths, enc_input, dec_input, cotangent, weights)
+    return grads[None].astype(F32)
 
 
 def solution(mesh):

time: 348 us -> 329 us (0.945)
  the two profiles are of different devices: /device:TPU:32 before, /device:TPU:1 now
where the time goes in v3:
time: 329 us; the launch traced here: 328 us
  Pallas kernels  323 us (98%)
  other arithmetic  4.19 us (1%)
    pallas_call x1, Pallas kernels, per_device(): pl.pallas_call(functools.partial(layer_kernel, 4096, float(tokens) ** (-0...  323 us

profile of v3, /device:TPU:1, one launch (start us, length us, event | category | flops | bytes accessed | tf_op | source)
XLA Modules:
  0.0 328.4 jit_solution(14436357309834392843)
XLA Ops:
  0.0 1.3 copy.6.lengths_ref
  1.3 322.9 %layers.1 = bf16[4,512,512]{2,1,0:T(8,128)(2,1)} custom-call(s32[4,1]{1,0:T(4,128)} %copy.6.lengths_ref, bf16[4,1,16,1024]{3,2,1,0:T(8,128)(2,1)} %enc_ref.1, bf16[4,1,16,1024]{3,2,1,0:T(8,128)(2,1)} %dec_ref.1, bf16[4,1,16,1024]{3,2,1,0:T(8,128)(2,1)} %cot_ref.1, bf16[1,4,512,512]{3,2,1,0:T(8,128)(2,1)} %weights_ref.1), custom_call_target="tpu_custom_call" | custom-call | tf_op jit(solution)/shard_map/layers/pallas_call | solution.py:762
  324.2 4.2 %bitcast_convert_fusion = f32[1,4,512,512]{3,2,1,0:T(8,128)} fusion(bf16[4,512,512]{2,1,0:T(8,128)(2,1)} %layers.1), kind=kLoop, calls=%fused_computation | loop fusion | flops 1048576 | bytes 6291456 | tf_op jit(solution)/shard_map/convert_element_type | solution.py:773

commit v4 on v3

--- a/solution.py
+++ b/solution.py
@@ -13,6 +13,7 @@
 BF = jnp.bfloat16
 F32 = jnp.float32
 MESH = pl.DeviceIdType.MESH
+SPREAD = 3
 ORDER = (2, 1, 3, 0)
 NT = (((1,), (1,)), ((), ()))
 NN = (((1,), (0,)), ((), ()))
@@ -26,9 +27,9 @@
 def layer_kernel(
     width, loss_scale,
     lengths_ref, enc_ref, dec_ref, cot_ref, weights_ref, out_ref,
-    w, xs, seed, seed_in, part, qrecv, qs, ks, vs, ps, rr, cs, oown, ost, orecv, xn,
+    w, wl, xs, sb, rb, tot, seed, seed_in, part, qrecv, qs, ks, vs, ps, rr, cs, oown, ost, orecv, xn,
     dpart, drecv, dd, cc, uown, ust, urecv, wown, wst, wrecv, gn, gein, geout, ob,
-    s_sem, ga_ss, ga_rs, gb_ss, gb_rs, gc_ss, gc_rs, i_ss, x_rs, f_ss, fp_ss, q_ss, q_rs, kv_ss, kv_rs,
+    s_sem, l_sem, rb_ss, rb_rs, cb_ss, cb_rs, xb_rs, xa_ss, xa_rs, ga_ss, ga_rs, gb_ss, gb_rs, gc_ss, gc_rs, i_ss, x_rs, f_ss, fp_ss, q_ss, q_rs, kv_ss, kv_rs,
     c_ss, c_rs, o_ss, o_rs, n_ss,
     d_ss, d_rs, dd_ss, dd_rs, cc_ss, cc_rs, u_ss, u_rs, w_ss, w_rs, e_ss, e_rs, gn_ss,
     b_ss, b_rs,
@@ -42,7 +43,8 @@
     odd = lax.rem(t, 2)
     decoder = s >= 4
     sel = jnp.where(decoder, 1, 0)
-    starts = (s == 0) | (s == 4) | (s == 7)
+    spread_out = s < SPREAD
+    starts = (s == 4) | (s == 7)
     other = (d, p + 1 - 2 * c)
 
     def place(tt, jj, ccc):
@@ -50,6 +52,9 @@
 
     def member(k):
         return place(t, lax.rem(j + k, 4), c)
+
+    def fellow(k):
+        return d, lax.rem(p + k, 4)
 
     def column(tt):
         return 2 * tt + lax.rem(d, 2), p
@@ -60,8 +65,14 @@
     across = column(lax.rem(t + 3 - 2 * odd, 4))
     senders = [place(k, p, d // 4) for k in range(4)]
     owner = [(4 * c + b, j) for b in range(4)]
+    heads_at = [place(q, p, e) for q in range(4) for e in range(2)]
+    heads_of = [(jnp.int32(k), j) for k in range(8)]
+    tokens_at = [place(p, jnp.int32(k), d // 4) for k in range(4)]
+    tokens_of = [(4 * c + b, t) for b in range(4)]
     start_to = [place(t, jnp.int32(k), p // 2) for k in range(4)]
     start_from = [(2 * t + a, 2 * c + e) for a in range(2) for e in range(2)]
+    first_to = [(2 * p + e, jnp.int32(k)) for k in range(4) for e in range(2)]
+    first_from = [(jnp.int32(k), d // 2) for k in range(8)]
 
     def same(dev):
         return (dev[0] == d) & (dev[1] == p)
@@ -112,7 +123,26 @@
     for k in range(1, 4):
         greet(member(k))
 
-    @pl.when(s > 0)
+    @pl.when(spread_out)
+    def _():
+        for k in range(1, 4):
+            greet(fellow(k))
+        for dev in heads_at + heads_of:
+            greet_other(dev)
+
+    @pl.when((s > 0) & spread_out)
+    def _():
+        for k in range(4):
+            greet(fellow(k), s - 1)
+        for dev in tokens_of:
+            greet_other(dev)
+
+    @pl.when(s == SPREAD)
+    def _():
+        for dev in tokens_of:
+            greet(dev, SPREAD - 1)
+
+    @pl.when(s > SPREAD)
     def _():
         for k in range(4):
             greet(member(k), s - 1)
@@ -130,6 +160,11 @@
         for e in range(2):
             greet_other((2 * t + e, j))
 
+    @pl.when(s == 0)
+    def _():
+        for dev in first_from:
+            greet_other(dev)
+
     @pl.when(starts)
     def _():
         for dev in start_from:
@@ -140,6 +175,9 @@
 
     count = 6 + jnp.where(s > 0, 4, 0) + jnp.where(s < 7, 4, 0) + others(owner)
     count = count + others([collector]) + jnp.where(starts, others(start_to), 0)
+    count = count + jnp.where(spread_out, 3 + others(heads_at) + others(heads_of), 0)
+    count = count + jnp.where((s > 0) & spread_out, others(tokens_at), 0)
+    count = count + jnp.where(s == 0, others(first_to), 0)
     pl.semaphore_wait(bar, count)
 
     def shards(piece, first, number):
@@ -158,7 +196,12 @@
         )
         return carry
 
-    lax.fori_loop(0, 8, give, 0)
+    local = pltpu.make_async_copy(weights_ref.at[0], wl, l_sem)
+
+    @pl.when(spread_out)
+    def _():
+        local.start()
+
 
     def begin(src_of, stream):
         for m in range(MICRO):
@@ -167,12 +210,17 @@
                     block = 2 * lax.rem(p, 2) + e
                     send_any(
                         src_of(m, e), xs.at[stream, m, block, lax.rem(d, 2)],
-                        i_ss.at[m, k], x_rs.at[stream, m, block], start_to[k],
+                        i_ss.at[m, 2 * k + e], x_rs.at[stream, m, block], start_to[k],
                     )
 
     @pl.when(s == 0)
     def _():
-        begin(lambda m, e: enc_ref.at[m, 0, :, pl.ds(512 * e, 512)], 0)
+        for m in range(MICRO):
+            for k in range(8):
+                send_any(
+                    enc_ref.at[m, 0, :, pl.ds(512 * (k % 2), 512)],
+                    ob.at[0, m, t, lax.rem(d, 2)], i_ss.at[m, k], xb_rs.at[m, t], first_to[k],
+                )
 
     @pl.when(s == 4)
     def _():
@@ -210,20 +258,25 @@
     def swapped(piece):
         arrived(shards(piece, 2 * odd, 2), gc_rs.at[piece])
 
-    def gather_most():
+    def gather(first, last):
+        lax.fori_loop(first, last, give, 0)
+
         @pl.when(inner)
         def _():
             def one(piece, carry):
                 collected(piece)
 
-                @pl.when(piece > 0)
+                @pl.when(piece > first)
                 def _():
                     pass_on(piece - 1)
 
                 return carry
 
-            lax.fori_loop(0, 7, one, 0)
-            collected(7)
+            lax.fori_loop(first, last, one, 0)
+
+            @pl.when(last > first)
+            def _():
+                pass_on(last - 1)
 
         @pl.when(jnp.logical_not(inner))
         def _():
@@ -235,19 +288,14 @@
                 swapped(piece)
                 return carry
 
-            lax.fori_loop(0, 6, one, 0)
-            lax.fori_loop(0, 6, other_one, 0)
-
-    def gather_one(piece):
-        @pl.when(inner)
-        def _():
-            pass_on(piece)
-
-        @pl.when(jnp.logical_not(inner))
-        def _():
-            swap(piece)
-
-    gather_most()
+            lax.fori_loop(first, last, one, 0)
+            lax.fori_loop(first, last, other_one, 0)
+
+    gather(0, jnp.where(spread_out, 0, 8))
+
+    @pl.when(spread_out)
+    def _():
+        local.wait()
 
     def rows(value):
         return value.reshape(32, 512)
@@ -314,17 +362,94 @@
                 xs.at[0, m, j], xs.at[0, m, j], fp_ss.at[m, k - 1], x_rs.at[0, m, j], member(k)
             ).start()
 
+    def project_first(m):
+        for k in ORDER:
+            quarter = lax.rem(p + 4 - k, 4)
+            arrived(ob.at[0, m, quarter], xb_rs.at[m, quarter])
+            left = rows(ob[0, m, quarter])
+            wide = left.astype(F32)
+            square = jnp.sum(wide * wide, axis=-1, keepdims=True)
+            high = square.astype(BF)
+            low = (square - high.astype(F32)).astype(BF)
+            for i in range(3):
+                sb[m, quarter, :, :, 512 * i:512 * i + 512] = dot(left, wl[i]).astype(BF).reshape(
+                    2, 16, 512
+                )
+            lane = lax.broadcasted_iota(jnp.int32, (32, 128), 1)
+            parts = jnp.where(
+                lane < 64, jnp.broadcast_to(high.astype(F32), (32, 128)),
+                jnp.broadcast_to(low.astype(F32), (32, 128)),
+            )
+            sb[m, quarter, :, :, 1536:] = parts.astype(BF).reshape(2, 16, 128)
+            for e in range(2):
+                send_any(
+                    sb.at[m, quarter, e], rb.at[m, d], rb_ss.at[m, 2 * quarter + e], rb_rs.at[m],
+                    place(quarter, p, e),
+                )
+
+    def output_first(m):
+        arrived(ob.at[3, m], cb_rs.at[m])
+        for k in ORDER:
+            term = dot(rows(ob[3, m, lax.rem(p + k, 4)]), wl[3], NT)
+            if k == 0:
+                oown[m] = term
+            else:
+                ost[m, k - 1] = term.astype(BF)
+                remote(
+                    ost.at[m, k - 1], orecv.at[m, k - 1], o_ss.at[m, k - 1], o_rs.at[m], fellow(k)
+                ).start()
+
+    def advance_first(m):
+        total = rows(ob[0, m, p]).astype(F32) + oown[m]
+        arrived(orecv.at[m], o_rs.at[m])
+        for k in range(3):
+            total = total + orecv[m, k].astype(F32)
+        xn[m] = total.astype(BF).reshape(2, 16, 512)
+
+        @pl.when(s < SPREAD - 1)
+        def _():
+            for k in ORDER:
+                remote(
+                    xn.at[m], ob.at[0, m, p], n_ss.at[m, k], xb_rs.at[m, p], fellow(k), s + 1
+                ).start()
+
+        @pl.when(s == SPREAD - 1)
+        def _():
+            block = lax.rem(d, 4)
+            for k in ORDER:
+                remote(
+                    xn.at[m], xs.at[0, m, block], n_ss.at[m, k], x_rs.at[0, m, block],
+                    place(p, lax.rem(j + k, 4), d // 4), s + 1,
+                ).start()
+
     def attend(m):
         @pl.when(decoder)
         def _():
             arrived(qrecv.at[m, :, pl.ds(0, 640)], q_rs.at[m])
             arrived(qrecv.at[m, :, pl.ds(640, 1152)], kv_rs.at[m])
 
-        @pl.when(jnp.logical_not(decoder))
+        @pl.when(jnp.logical_not(decoder | spread_out))
         def _():
             arrived(qrecv.at[m], q_rs.at[m])
 
-        total = part[m, c] + qrecv[m]
+        @pl.when(jnp.logical_not(spread_out))
+        def _():
+            tot[...] = part[m, c] + qrecv[m]
+
+        @pl.when(spread_out)
+        def _():
+            arrived(rb.at[m], rb_rs.at[m])
+            summed = rb[m, 0].astype(F32)
+            for k in range(1, 8):
+                summed = summed + rb[m, k].astype(F32)
+            square = summed[:, 1536:1537] + summed[:, 1600:1601]
+            square = jnp.broadcast_to(square, (16, 128))
+            tot[:, :512] = summed[:, :512]
+            tot[:, 512:640] = square
+            tot[:, 640:1664] = summed[:, 512:1536]
+            tot[:, 1664:] = square
+
+        total = tot[...]
         factor_q = lax.rsqrt(total[:, 512:513] * (1.0 / width) + EPSILON)
         factor_k = lax.rsqrt(total[:, 1664:1665] * (1.0 / width) + EPSILON)
         rr[m, 0] = jnp.broadcast_to(factor_q, (16, 128))
@@ -343,24 +468,30 @@
             ps[m, h] = weight.astype(F32)
             contexts.append(dot(weight, value[:, cols]).astype(BF))
         cs[m, c] = jnp.concatenate(contexts, axis=1)
-        remote(cs.at[m, c], cs.at[m, c], c_ss.at[m], c_rs.at[m], other).start()
+
+        @pl.when(jnp.logical_not(spread_out))
+        def _():
+            remote(cs.at[m, c], cs.at[m, c], c_ss.at[m], c_rs.at[m], other).start()
+
+        @pl.when(spread_out)
+        def _():
+            for k in range(8):
+                send_any(
+                    cs.at[m, c], ob.at[3, m, t, c], cb_ss.at[m, k], cb_rs.at[m], heads_of[k]
+                )
 
     def output(m):
         arrived(cs.at[m, c], c_rs.at[m])
-
-        @pl.when(s < 7)
-        def _():
-            context = rows(cs[m])
-            for k in ORDER:
-                term = dot(context, w[3, lax.rem(j + k, 4)], NT)
-                if k == 0:
-                    oown[m] = term
-                else:
-                    ost[m, k - 1] = term.astype(BF)
-                    remote(
-                        ost.at[m, k - 1], orecv.at[m, k - 1], o_ss.at[m, k - 1], o_rs.at[m],
-                        member(k),
-                    ).start()
+        context = rows(cs[m])
+        for k in ORDER:
+            term = dot(context, w[3, lax.rem(j + k, 4)], NT)
+            if k == 0:
+                oown[m] = term
+            else:
+                ost[m, k - 1] = term.astype(BF)
+                remote(
+                    ost.at[m, k - 1], orecv.at[m, k - 1], o_ss.at[m, k - 1], o_rs.at[m], member(k)
+                ).start()
 
     def advance(m):
         total = rows(xs[sel, m, j]).astype(F32) + oown[m]
@@ -374,7 +505,19 @@
             ).start()
 
     def forward_step(i):
-        @pl.when((i < MICRO) & (s < 4) & (s > 0))
+        @pl.when((i < MICRO) & spread_out)
+        def _():
+            project_first(i)
+
+        @pl.when((i > 2) & spread_out)
+        def _():
+            advance_first(i - 3)
+
+        @pl.when((i > 1) & (i < MICRO + 2) & spread_out)
+        def _():
+            output_first(i - 2)
+
+        @pl.when((i < MICRO) & jnp.logical_not(decoder | spread_out))
         def _():
             project_all(i)
 
@@ -394,16 +537,18 @@
             def _():
                 relay(i + 2)
 
-        @pl.when((i > 0) & (s < 7))
+        @pl.when((i > 0) & (i <= MICRO) & (s >= SPREAD) & (s < 7))
         def _():
             advance(i - 1)
 
-        @pl.when(i < MICRO)
-        def _():
-            @pl.when(s > 0)
-            def _():
-                attend(i)
-
+        late = jnp.where(spread_out, 1, 0)
+
+        @pl.when((i >= late) & (i < MICRO + late))
+        def _():
+            attend(i - late)
+
+        @pl.when((i < MICRO) & (s >= SPREAD) & (s < 7))
+        def _():
             output(i)
 
     def to_owners(src_of, slot, m=None):
@@ -451,6 +596,8 @@
         cc[m, 0, c] = jnp.broadcast_to(means[0] * factors[0] * factors[0], (16, 128))
         cc[m, 1, c] = jnp.broadcast_to((means[1] + means[2]) * factors[1] * factors[1], (16, 128))
         remote(cc.at[m, :, c], cc.at[m, :, c], cc_ss.at[m], cc_rs.at[m], other).start()
+
+    def spread_back(m):
         arrived(dd.at[m, :, c], dd_rs.at[m])
         arrived(cc.at[m, :, c], cc_rs.at[m])
 
@@ -522,6 +669,10 @@
         def _():
             project_back(i)
 
+        @pl.when((i < MICRO) & (s < 4))
+        def _():
+            attend_back(i)
+
         @pl.when((i > 0) & (s > 0) & (s != 4))
         def _():
             advance_back(i - 1)
@@ -530,9 +681,13 @@
         def _():
             advance_key(i - 1)
 
+        @pl.when((i < MICRO) & (s >= 4))
+        def _():
+            attend_back(i)
+
         @pl.when(i < MICRO)
         def _():
-            attend_back(i)
+            spread_back(i)
 
             @pl.when(s < 2)
             def _():
@@ -544,28 +699,47 @@
         def _():
             advance_key(i - 1)
 
-    def early(what):
-        @pl.when(s == 0)
-        def _():
-            def one(m, carry):
-                what(m)
-                return carry
-
-            lax.fori_loop(0, MICRO, one, 0)
-
-    early(project_all)
-    gather_one(6)
-    early(attend)
-    gather_one(7)
-
-    @pl.when(jnp.logical_not(inner))
-    def _():
-        swapped(6)
-        swapped(7)
+    def last_step(i):
+        @pl.when(i < MICRO)
+        def _():
+            project_query(i)
+
+        @pl.when(i > 0)
+        def _():
+            advance_back(i - 1)
+
+        @pl.when(i < MICRO)
+        def _():
+            attend(i)
+            attend_back(i)
+
+        @pl.when(i < MICRO - 1)
+        def _():
+            project_key(i + 1)
+
+        @pl.when(i < MICRO)
+        def _():
+            spread_back(i)
+
+        @pl.when(i < MICRO - 2)
+        def _():
+            relay(i + 2)
+
+        @pl.when(i > 0)
+        def _():
+            advance_key(i - 1)
 
     @pl.when(s == 4)
     def _():
         project_query(0)
+
+    @pl.when(s == 7)
+    def _():
+        def one(m, carry):
+            project_back(m)
+            return carry
+
+        lax.fori_loop(0, MICRO, one, 0)
 
     @pl.when(s > 4)
     def _():
@@ -573,30 +747,45 @@
         relay(1)
         project_key(0)
 
+    def forward_to_owners():
+        to_owners(lambda b: xs.at[sel, :, b], 0)
+        to_owners(lambda b: cs, 3)
+
     def step(n, carry):
-        @pl.when(n <= MICRO)
+        @pl.when((s == 7) & (n <= MICRO))
+        def _():
+            last_step(n)
+
+        @pl.when((s < 7) & (n <= MICRO + 2))
         def _():
             forward_step(n)
 
-        @pl.when(n == MICRO + 1)
-        def _():
-            to_owners(lambda b: xs.at[sel, :, b], 0)
-
-            @pl.when(decoder)
+        @pl.when(n == MICRO + 3)
+        def _():
+            @pl.when(s == SPREAD)
             def _():
-                to_owners(lambda b: xs.at[0, :, b], 1)
-
-            to_owners(lambda b: cs, 3)
-
-        back = n - jnp.where(s == 7, 0, MICRO + 1)
-
-        @pl.when((back >= 0) & (back <= MICRO))
-        def _():
-            backward_step(back)
+                forward_to_owners()
+
+            @pl.when((s > 0) & spread_out)
+            def _():
+                for k in range(4):
+                    send_any(
+                        ob.at[0, :, p], xs.at[0, :, lax.rem(d, 4)], xa_ss.at[k], xa_rs, tokens_at[k]
+                    )
+
+            gather(0, jnp.where(spread_out, 8, 0))
+
+            @pl.when((s > 0) & spread_out)
+            def _():
+                arrived(xs.at[0], xa_rs)
+
+        @pl.when((s < 7) & (n >= MICRO + 3))
+        def _():
+            backward_step(n - MICRO - 3)
 
         return carry
 
-    lax.fori_loop(0, 2 * MICRO + 2, step, 0)
+    lax.fori_loop(0, 2 * MICRO + 4, step, 0)
 
     @pl.when(s > 1)
     def _():
@@ -604,11 +793,28 @@
         for i in range(3):
             to_owners(lambda b: dd.at[:, i], 4 + i)
 
+    @pl.when(decoder)
+    def _():
+        @pl.when(s == 7)
+        def _():
+            for m in range(MICRO):
+                arrived(cs.at[m, c], c_rs.at[m])
+
+        forward_to_owners()
+        to_owners(lambda b: xs.at[0, :, b], 1)
+
     key_slot = jnp.where(decoder, 1, 0)
-    arrived(ob.at[3], b_rs.at[3])
+
+    @pl.when(s >= SPREAD)
+    def _():
+        arrived(ob.at[3], b_rs.at[3])
+
     arrived(ob.at[2], b_rs.at[2])
     out_ref[3] = dot(ob[2].reshape(512, 512), ob[3].reshape(512, 512), TN).astype(BF)
-    arrived(ob.at[0], b_rs.at[0])
+
+    @pl.when(s >= SPREAD)
+    def _():
+        arrived(ob.at[0], b_rs.at[0])
 
     @pl.when(decoder)
     def _():
@@ -622,8 +828,19 @@
     @pl.when(starts)
     def _():
         for m in range(MICRO):
-            for k in range(4):
-                sent_any(seed.at[m], i_ss.at[m, k], start_to[k])
+            for k in range(8):
+                sent_any(seed.at[m, 0], i_ss.at[m, k], start_to[k // 2])
+
+    @pl.when(s == 0)
+    def _():
+        for m in range(MICRO):
+            for k in range(8):
+                sent_any(seed.at[m, 0], i_ss.at[m, k], first_to[k])
+
+    @pl.when((s > 0) & spread_out)
+    def _():
+        for k in range(4):
+            sent_any(ob.at[0, :, 0], xa_ss.at[k], tokens_at[k])
 
     def given(piece, carry):
         sent_any(own_shard(piece), ga_ss.at[piece], collector)
@@ -638,14 +855,17 @@
 
     lax.fori_loop(0, 8, given, 0)
 
-    owners_sent(lambda b: xs.at[sel, :, b], 0)
+
+    @pl.when(s >= SPREAD)
+    def _():
+        owners_sent(lambda b: xs.at[sel, :, b], 0)
+        owners_sent(lambda b: cs, 3)
 
     @pl.when(decoder)
     def _():
         owners_sent(lambda b: xs.at[0, :, b], 1)
 
     owners_sent(lambda b: xs.at[2, :, b], 2)
-    owners_sent(lambda b: cs, 3)
     for i in range(3):
         owners_sent(lambda b: dd.at[:, i], 4 + i)
 
@@ -655,11 +875,20 @@
             arrived(part.at[m, 0, :, pl.ds(0, 640)], q_ss.at[m])
             arrived(part.at[m, 0, :, pl.ds(640, 1152)], kv_ss.at[m])
 
-        @pl.when(jnp.logical_not(decoder))
+        @pl.when(jnp.logical_not(decoder | spread_out))
         def _():
             arrived(part.at[m, 0], q_ss.at[m])
 
-        arrived(cs.at[m, 0], c_ss.at[m])
+        @pl.when(jnp.logical_not(spread_out))
+        def _():
+            arrived(cs.at[m, 0], c_ss.at[m])
+
+        @pl.when(spread_out)
+        def _():
+            for k in range(8):
+                sent_any(sb.at[m, 0, 0], rb_ss.at[m, k], heads_at[k])
+                sent_any(cs.at[m, 0], cb_ss.at[m, k], heads_of[k])
+
         arrived(dpart.at[m, 0], d_ss.at[m])
         arrived(dd.at[m, :, 0], dd_ss.at[m])
         arrived(cc.at[m, :, 0], cc_ss.at[m])
@@ -710,7 +939,11 @@
     tile = (2, 16, 512)
     scratch = [
         pltpu.VMEM((4, 4, 512, 512), BF),
+        pltpu.VMEM((4, 512, 512), BF),
         pltpu.VMEM((3, MICRO, 4) + tile, BF),
+        pltpu.VMEM((MICRO, 4, 2, 16, 1664), BF),
+        pltpu.VMEM((MICRO, 8, 16, 1664), BF),
+        pltpu.VMEM((16, 1792), F32),
         pltpu.VMEM((MICRO, 2, 16, 512), BF),
         pltpu.VMEM((MICRO, 16, 1024), BF),
         pltpu.VMEM((MICRO, 2, 16, 1792), F32),
@@ -739,11 +972,14 @@
         pltpu.VMEM((MICRO,) + tile, BF),
         pltpu.VMEM((MICRO,) + tile, BF),
         pltpu.VMEM((7, MICRO, 4) + tile, BF),
-        dma,
+        dma, dma,
+        dma((MICRO, 8)), dma((MICRO,)),
+        dma((MICRO, 8)), dma((MICRO,)),
+        dma((MICRO, 4)), dma((4,)), dma,
         dma((8,)), dma((8,)),
         dma((8, 2)), dma((8,)),
         dma((8,)), dma((8,)),
-        dma((MICRO, 4)), dma((3, MICRO, 4)),
+        dma((MICRO, 8)), dma((3, MICRO, 4)),
         dma((MICRO,)), dma((MICRO, 3)),
         dma((MICRO,)), dma((MICRO,)),
         dma((MICRO,)), dma((MICRO,)),

time: 329 us -> 300 us (0.912)
  Pallas kernels: 323 us -> 294 us
    pallas_call x1, Pallas kernels: 323 us -> 294 us  [per_device(): pl.pallas_call(functools.partial(layer_kernel, 4096, float(tokens) ** (-0...]
where the time goes in v4:
time: 300 us
  Pallas kernels  294 us (98%)
  other arithmetic  4.19 us (1%)
    pallas_call x1, Pallas kernels, per_device(): pl.pallas_call(functools.partial(layer_kernel, 4096, float(tokens) ** (-0...  294 us

profile of v4, /device:TPU:1, one launch (start us, length us, event | category | flops | bytes accessed | tf_op | source)
XLA Modules:
  0.0 299.9 jit_solution(3466632284987402629)
XLA Ops:
  0.0 1.3 copy.6.lengths_ref
  1.3 294.4 %layers.1 = bf16[4,512,512]{2,1,0:T(8,128)(2,1)} custom-call(s32[4,1]{1,0:T(4,128)} %copy.6.lengths_ref, bf16[4,1,16,1024]{3,2,1,0:T(8,128)(2,1)} %enc_ref.1, bf16[4,1,16,1024]{3,2,1,0:T(8,128)(2,1)} %dec_ref.1, bf16[4,1,16,1024]{3,2,1,0:T(8,128)(2,1)} %cot_ref.1, bf16[1,4,512,512]{3,2,1,0:T(8,128)(2,1)} %weights_ref.1), custom_call_target="tpu_custom_call" | custom-call | tf_op jit(solution)/shard_map/layers/pallas_call | solution.py:998
  295.7 4.2 %bitcast_convert_fusion = f32[1,4,512,512]{3,2,1,0:T(8,128)} fusion(bf16[4,512,512]{2,1,0:T(8,128)(2,1)} %layers.1), kind=kLoop, calls=%fused_computation | loop fusion | flops 1048576 | bytes 6291456 | tf_op jit(solution)/shard_map/convert_element_type | solution.py:1009

commit v5 on v4

--- a/solution.py
+++ b/solution.py
@@ -13,7 +13,7 @@
 BF = jnp.bfloat16
 F32 = jnp.float32
 MESH = pl.DeviceIdType.MESH
-SPREAD = 3
+SPREAD = 2
 ORDER = (2, 1, 3, 0)
 NT = (((1,), (1,)), ((), ()))
 NN = (((1,), (0,)), ((), ()))
@@ -27,7 +27,7 @@
 def layer_kernel(
     width, loss_scale,
     lengths_ref, enc_ref, dec_ref, cot_ref, weights_ref, out_ref,
-    w, wl, xs, sb, rb, tot, seed, seed_in, part, qrecv, qs, ks, vs, ps, rr, cs, oown, ost, orecv, xn,
+    w, wt, wl, xs, sb, rb, tot, seed, seed_in, part, qrecv, qs, ks, vs, ps, rr, cs, oown, ost, orecv, xn,
     dpart, drecv, dd, cc, uown, ust, urecv, wown, wst, wrecv, gn, gein, geout, ob,
     s_sem, l_sem, rb_ss, rb_rs, cb_ss, cb_rs, xb_rs, xa_ss, xa_rs, ga_ss, ga_rs, gb_ss, gb_rs, gc_ss, gc_rs, i_ss, x_rs, f_ss, fp_ss, q_ss, q_rs, kv_ss, kv_rs,
     c_ss, c_rs, o_ss, o_rs, n_ss,
@@ -189,12 +189,11 @@
     def own_shard(piece):
         return weights_ref.at[0, piece // 2, pl.ds(256 * lax.rem(piece, 2), 256)]
 
-    def give(piece, carry):
+    def give(piece):
         send_any(
             own_shard(piece), shard(piece, lax.rem(d, 4)), ga_ss.at[piece], ga_rs.at[piece],
             collector,
         )
-        return carry
 
     local = pltpu.make_async_copy(weights_ref.at[0], wl, l_sem)
 
@@ -258,40 +257,45 @@
     def swapped(piece):
         arrived(shards(piece, 2 * odd, 2), gc_rs.at[piece])
 
-    def gather(first, last):
-        lax.fori_loop(first, last, give, 0)
+    def when(cond, what, *args):
+        @pl.when(cond)
+        def _():
+            what(*args)
+
+    def repeat(first, last, what):
+        def one(piece, carry):
+            what(piece)
+            return carry
+
+        lax.fori_loop(first, last, one, 0)
+
+    def collect_on(piece):
+        collected(piece)
+        when(piece > 0, pass_on, piece - 1)
+
+    def gather_some(pieces):
+        repeat(0, 8, give)
 
         @pl.when(inner)
         def _():
-            def one(piece, carry):
-                collected(piece)
-
-                @pl.when(piece > first)
-                def _():
-                    pass_on(piece - 1)
-
-                return carry
-
-            lax.fori_loop(first, last, one, 0)
-
-            @pl.when(last > first)
-            def _():
-                pass_on(last - 1)
+            repeat(0, pieces + 1, collect_on)
+            repeat(pieces + 1, 8, collected)
 
         @pl.when(jnp.logical_not(inner))
         def _():
-            def one(piece, carry):
-                swap(piece)
-                return carry
-
-            def other_one(piece, carry):
-                swapped(piece)
-                return carry
-
-            lax.fori_loop(first, last, one, 0)
-            lax.fori_loop(first, last, other_one, 0)
-
-    gather(0, jnp.where(spread_out, 0, 8))
+            repeat(0, pieces, swap)
+            repeat(0, pieces, swapped)
+
+    def gather_one(piece):
+        when(inner, pass_on, piece)
+        when(jnp.logical_not(inner), swap, piece)
+
+    def gather_end(pieces):
+        @pl.when(jnp.logical_not(inner))
+        def _():
+            repeat(pieces, 8, swapped)
+
+    when(jnp.logical_not(spread_out), gather_some, 6)
 
     @pl.when(spread_out)
     def _():
@@ -517,7 +521,9 @@
         def _():
             output_first(i - 2)
 
-        @pl.when((i < MICRO) & jnp.logical_not(decoder | spread_out))
+        begun = jnp.where(s == SPREAD, 2, 0)
+
+        @pl.when((i >= begun) & (i < MICRO) & jnp.logical_not(decoder | spread_out))
         def _():
             project_all(i)
 
@@ -543,7 +549,7 @@
 
         late = jnp.where(spread_out, 1, 0)
 
-        @pl.when((i >= late) & (i < MICRO + late))
+        @pl.when((i >= jnp.where(s == SPREAD, 1, late)) & (i < MICRO + late))
         def _():
             attend(i - late)
 
@@ -608,7 +614,7 @@
                 block = lax.rem(j + k, 4)
                 term = -rows(xs[stream, m, block]).astype(F32) * shift
                 for i, left in zip(pairs, lefts):
-                    term = term + dot(left, w[i, block], NT)
+                    term = term + dot(left, wt[i, block])
                 if k == 0:
                     own[m] = term
                 else:
@@ -729,6 +735,24 @@
         def _():
             advance_key(i - 1)
 
+    @pl.when(jnp.logical_not(spread_out))
+    def _():
+        when(s == SPREAD, project_all, 0)
+        gather_one(6)
+
+        @pl.when(s == SPREAD)
+        def _():
+            attend(0)
+            project_all(1)
+
+        gather_one(7)
+        gather_end(6)
+
+    def turn(which):
+        wt[which // 4, lax.rem(which, 4)] = w[which // 4, lax.rem(which, 4)].T
+
+    when(decoder, repeat, 0, 12, turn)
+
     @pl.when(s == 4)
     def _():
         project_query(0)
@@ -762,7 +786,7 @@
 
         @pl.when(n == MICRO + 3)
         def _():
-            @pl.when(s == SPREAD)
+            @pl.when((s >= SPREAD) & (s < 4))
             def _():
                 forward_to_owners()
 
@@ -773,7 +797,14 @@
                         ob.at[0, :, p], xs.at[0, :, lax.rem(d, 4)], xa_ss.at[k], xa_rs, tokens_at[k]
                     )
 
-            gather(0, jnp.where(spread_out, 8, 0))
+            @pl.when(spread_out)
+            def _():
+                gather_some(6)
+                gather_one(6)
+                gather_one(7)
+                gather_end(6)
+
+            when((s > 0) & (s < 4), repeat, 0, 12, turn)
 
             @pl.when((s > 0) & spread_out)
             def _():
@@ -939,6 +970,7 @@
     tile = (2, 16, 512)
     scratch = [
         pltpu.VMEM((4, 4, 512, 512), BF),
+        pltpu.VMEM((3, 4, 512, 512), BF),
         pltpu.VMEM((4, 512, 512), BF),
         pltpu.VMEM((3, MICRO, 4) + tile, BF),
         pltpu.VMEM((MICRO, 4, 2, 16, 1664), BF),

time: 300 us -> 296 us (0.987)
  Pallas kernels: 294 us -> 291 us
    pallas_call x1, Pallas kernels: 294 us -> 291 us  [per_device(): pl.pallas_call(functools.partial(layer_kernel, 4096, float(tokens) ** (-0...]
where the time goes in v5:
time: 296 us
  Pallas kernels  291 us (98%)
  other arithmetic  4.19 us (1%)
    pallas_call x1, Pallas kernels, per_device(): pl.pallas_call(functools.partial(layer_kernel, 4096, float(tokens) ** (-0...  291 us

profile of v5, /device:TPU:1, one launch (start us, length us, event | category | flops | bytes accessed | tf_op | source)
XLA Modules:
  0.0 296.2 jit_solution(11015173747481348596)
XLA Ops:
  0.0 1.3 copy.6.lengths_ref
  1.3 290.7 %layers.1 = bf16[4,512,512]{2,1,0:T(8,128)(2,1)} custom-call(s32[4,1]{1,0:T(4,128)} %copy.6.lengths_ref, bf16[4,1,16,1024]{3,2,1,0:T(8,128)(2,1)} %enc_ref.1, bf16[4,1,16,1024]{3,2,1,0:T(8,128)(2,1)} %dec_ref.1, bf16[4,1,16,1024]{3,2,1,0:T(8,128)(2,1)} %cot_ref.1, bf16[1,4,512,512]{3,2,1,0:T(8,128)(2,1)} %weights_ref.1), custom_call_target="tpu_custom_call" | custom-call | tf_op jit(solution)/shard_map/layers/pallas_call | solution.py:1030
  292.0 4.2 %bitcast_convert_fusion = f32[1,4,512,512]{3,2,1,0:T(8,128)} fusion(bf16[4,512,512]{2,1,0:T(8,128)(2,1)} %layers.1), kind=kLoop, calls=%fused_computation | loop fusion | flops 1048576 | bytes 6291456 | tf_op jit(solution)/shard_map/convert_element_type | solution.py:1041

commit v6 on v5

--- a/solution.py
+++ b/solution.py
@@ -695,7 +695,7 @@
         def _():
             spread_back(i)
 
-            @pl.when(s < 2)
+            @pl.when((s == 0) | ((s == 1) & (i < 2)))
             def _():
                 to_owners(lambda b: xs.at[2, i, b], 2, i)
                 for k in range(3):
@@ -817,6 +817,13 @@
         return carry
 
     lax.fori_loop(0, 2 * MICRO + 4, step, 0)
+
+    @pl.when(s == 1)
+    def _():
+        for m in range(2, MICRO):
+            to_owners(lambda b: xs.at[2, m, b], 2, m)
+            for i in range(3):
+                to_owners(lambda b: dd.at[m, i], 4 + i, m)
 
     @pl.when(s > 1)
     def _():

time: 296 us -> 295 us (level)
  no operation moved by 1% of the time
where the time goes in v6:
time: 295 us
  Pallas kernels  290 us (98%)
  other arithmetic  4.19 us (1%)
    pallas_call x1, Pallas kernels, per_device(): pl.pallas_call(functools.partial(layer_kernel, 4096, float(tokens) ** (-0...  290 us

profile of v6, /device:TPU:1, one launch (start us, length us, event | category | flops | bytes accessed | tf_op | source)
XLA Modules:
  0.0 295.3 jit_solution(10568442237637083378)
XLA Ops:
  0.0 1.3 copy.6.lengths_ref
  1.3 289.8 %layers.1 = bf16[4,512,512]{2,1,0:T(8,128)(2,1)} custom-call(s32[4,1]{1,0:T(4,128)} %copy.6.lengths_ref, bf16[4,1,16,1024]{3,2,1,0:T(8,128)(2,1)} %enc_ref.1, bf16[4,1,16,1024]{3,2,1,0:T(8,128)(2,1)} %dec_ref.1, bf16[4,1,16,1024]{3,2,1,0:T(8,128)(2,1)} %cot_ref.1, bf16[1,4,512,512]{3,2,1,0:T(8,128)(2,1)} %weights_ref.1), custom_call_target="tpu_custom_call" | custom-call | tf_op jit(solution)/shard_map/layers/pallas_call | solution.py:1037
  291.1 4.2 %bitcast_convert_fusion = f32[1,4,512,512]{3,2,1,0:T(8,128)} fusion(bf16[4,512,512]{2,1,0:T(8,128)(2,1)} %layers.1), kind=kLoop, calls=%fused_computation | loop fusion | flops 1048576 | bytes 6291456 | tf_op jit(solution)/shard_map/convert_element_type | solution.py:1048

commit v7 on v6

--- a/solution.py
+++ b/solution.py
@@ -531,17 +531,17 @@
         def _():
             project_query(i + 1)
 
+        @pl.when((i < MICRO) & (s > 4))
+        def _():
+            project_query(i)
+
         @pl.when(((i < MICRO) & (s == 4)) | ((i < MICRO - 1) & (s > 4)))
         def _():
             project_key(i + jnp.where(s > 4, 1, 0))
 
-        @pl.when((i < MICRO) & (s > 4))
-        def _():
-            project_query(i)
-
-            @pl.when(i < MICRO - 2)
-            def _():
-                relay(i + 2)
+        @pl.when((i < MICRO - 2) & (s > 4))
+        def _():
+            relay(i + 2)
 
         @pl.when((i > 0) & (i <= MICRO) & (s >= SPREAD) & (s < 7))
         def _():

time: 295 us -> 297 us (level)
  no operation moved by 1% of the time
where the time goes in v7:
time: 297 us
  Pallas kernels  292 us (98%)
  other arithmetic  4.19 us (1%)
    pallas_call x1, Pallas kernels, per_device(): pl.pallas_call(functools.partial(layer_kernel, 4096, float(tokens) ** (-0...  292 us

profile of v7, /device:TPU:1, one launch (start us, length us, event | category | flops | bytes accessed | tf_op | source)
XLA Modules:
  0.0 297.2 jit_solution(15202364695562241610)
XLA Ops:
  0.0 1.3 copy.6.lengths_ref
  1.3 291.6 %layers.1 = bf16[4,512,512]{2,1,0:T(8,128)(2,1)} custom-call(s32[4,1]{1,0:T(4,128)} %copy.6.lengths_ref, bf16[4,1,16,1024]{3,2,1,0:T(8,128)(2,1)} %enc_ref.1, bf16[4,1,16,1024]{3,2,1,0:T(8,128)(2,1)} %dec_ref.1, bf16[4,1,16,1024]{3,2,1,0:T(8,128)(2,1)} %cot_ref.1, bf16[1,4,512,512]{3,2,1,0:T(8,128)(2,1)} %weights_ref.1), custom_call_target="tpu_custom_call" | custom-call | tf_op jit(solution)/shard_map/layers/pallas_call | solution.py:1037
  293.0 4.2 %bitcast_convert_fusion = f32[1,4,512,512]{3,2,1,0:T(8,128)} fusion(bf16[4,512,512]{2,1,0:T(8,128)(2,1)} %layers.1), kind=kLoop, calls=%fused_computation | loop fusion | flops 1048576 | bytes 6291456 | tf_op jit(solution)/shard_map/convert_element_type | solution.py:1048
